TPU v7x, 256 devices: a whole 4x4x8 slice. The times are simulated.
256 devices in a mesh: dp: 16 (over z_hi, y), ctx: 16 (over x, z_lo, core).
Axes of the slice: x: 4, y: 4, z: 8 (z_hi: 4, z_lo: 2; z = z_hi * 2 + z_lo), core: 2. Of those that a mesh axis runs over, the one named last changes fastest.
Arguments:
- value_in: float32 [16, 128, 4096], P('dp', None, 'ctx'), may hold values from -6 to 6
- key_in: float32 [16, 128, 4096], P('dp', None, 'ctx'), may hold values from -6 to 6
- query_in: float32 [16, 128, 4096], P('dp', None, 'ctx'), may hold values from -6 to 6
- cotangent: float32 [16, 128, 4096], P('dp', None, 'ctx'), may hold values from -6 to 6
- filter_param: float32 [128, 4096], P(None, 'ctx'), may hold values from -6 to 6
Outputs:
- query_grad: float32 [16, 128, 4096], P('dp', None, 'ctx')
- key_grad: float32 [16, 128, 4096], P('dp', None, 'ctx')
- value_grad: float32 [16, 128, 4096], P('dp', None, 'ctx')
- filter_grad: float32 [128, 4096], P(None, 'ctx')
All inputs are finite; a program needn't handle non-finite values.
Results may differ from a plain program's by a relative error of at most 0.0003.
Values sent between devices are 32-bit elements; how exact they have to be, the bound alone decides.
No kernel may reach another device: no remote copies, remote signals or barrier semaphores. Data moves between devices by JAX's collectives and lax.ppermute only.
A program may use at most 64 MiB of HBM per device.

v0:
```python
import math

import jax
import jax.numpy as jnp
from jax import lax
from jax.sharding import PartitionSpec as P

exact_mode = lax.Precision.HIGHEST


def counter(extent):
    return lax.iota(jnp.int32, extent)


def phase_grid(left_index, right_index, period):
    product = left_index[:, None] * right_index[None, :] % period
    angles = product.astype(jnp.float32) * (2.0 * math.pi / period)
    return (jnp.cos(angles), jnp.sin(angles))


def rotate(real_part, imag_part, cosine, sine, inverse):
    if inverse:
        return (real_part * cosine - imag_part * sine, imag_part * cosine + real_part * sine)
    return (real_part * cosine + imag_part * sine, imag_part * cosine - real_part * sine)


def mix(formula, cosine, sine, real_part, imag_part, inverse):

    def contract(table, values):
        return jnp.einsum(formula, table, values, precision=exact_mode)

    if inverse:
        return (
            contract(cosine, real_part) - contract(sine, imag_part),
            contract(cosine, imag_part) + contract(sine, real_part),
        )
    return (
        contract(cosine, real_part) + contract(sine, imag_part),
        contract(cosine, imag_part) - contract(sine, real_part),
    )


def forward_spectrum(signal):
    groups = lax.axis_size("ctx")
    rows = signal.shape[0]
    extent = signal.shape[1]
    stride = extent // groups
    total = 2 * groups * extent
    outer = extent // 128
    columns = lax.all_to_all(signal[:, None, :], "ctx", split_axis=2, concat_axis=1, tiled=True)
    cosine, sine = phase_grid(counter(2 * groups), counter(groups), 2 * groups)
    real_part = jnp.einsum("kc,bcr->bkr", cosine, columns, precision=exact_mode)
    imag_part = -jnp.einsum("kc,bcr->bkr", sine, columns, precision=exact_mode)
    positions = lax.axis_index("ctx") * stride + counter(stride)
    cosine, sine = phase_grid(counter(2 * groups), positions, total)
    real_part, imag_part = rotate(real_part, imag_part, cosine, sine, False)
    spread = lax.all_to_all(
        jnp.stack([real_part, imag_part]), "ctx", split_axis=2, concat_axis=3, tiled=True
    )
    real_part = spread[0].reshape(rows, 2, outer, 128)
    imag_part = spread[1].reshape(rows, 2, outer, 128)
    cosine, sine = phase_grid(counter(outer), counter(outer), outer)
    real_part, imag_part = mix("kb,xeba->xeka", cosine, sine, real_part, imag_part, False)
    cosine, sine = phase_grid(counter(outer), counter(128), extent)
    real_part, imag_part = rotate(real_part, imag_part, cosine, sine, False)
    cosine, sine = phase_grid(counter(128), counter(128), 128)
    return mix("ja,xeka->xekj", cosine, sine, real_part, imag_part, False)


def inverse_signal(real_part, imag_part):
    groups = lax.axis_size("ctx")
    rows = real_part.shape[0]
    outer = real_part.shape[2]
    extent = outer * 128
    total = 2 * groups * extent
    cosine, sine = phase_grid(counter(128), counter(128), 128)
    real_part, imag_part = mix("aj,xekj->xeka", cosine, sine, real_part, imag_part, True)
    cosine, sine = phase_grid(counter(outer), counter(128), extent)
    real_part, imag_part = rotate(real_part, imag_part, cosine, sine, True)
    cosine, sine = phase_grid(counter(outer), counter(outer), outer)
    real_part, imag_part = mix("bk,xeka->xeba", cosine, sine, real_part, imag_part, True)
    real_part = real_part.reshape(rows, 2, extent)
    imag_part = imag_part.reshape(rows, 2, extent)
    frequency = 2 * lax.axis_index("ctx") + counter(2)
    cosine, sine = phase_grid(frequency, counter(extent), total)
    real_part, imag_part = rotate(real_part, imag_part, cosine, sine, True)
    gathered = lax.all_to_all(
        jnp.stack([real_part, imag_part]), "ctx", split_axis=3, concat_axis=2, tiled=True
    )
    cosine, sine = phase_grid(counter(groups), counter(2 * groups), 2 * groups)

    def contract(table, values):
        return jnp.einsum("ck,bkr->bcr", table, values, precision=exact_mode)

    results = [contract(cosine, gathered[0]) - contract(sine, gathered[1])]
    stacked = jnp.stack(results) * (1.0 / total)
    returned = lax.all_to_all(stacked, "ctx", split_axis=2, concat_axis=3, tiled=True)
    return returned[:, :, 0, :]


def multiply_spectra(first, second, conjugate):
    first_real, first_imag = first
    second_real, second_imag = second
    if conjugate:
        second_imag = -second_imag
    return (
        first_real * second_real - first_imag * second_imag,
        first_real * second_imag + first_imag * second_real,
    )


def run_inverse(spectra, channels):
    count = len(spectra)
    all_real = jnp.concatenate([entry[0] for entry in spectra], 0)
    all_imag = jnp.concatenate([entry[1] for entry in spectra], 0)
    signals = inverse_signal(all_real, all_imag)
    return [signals[0, index * channels : (index + 1) * channels] for index in range(count)]


def on_device(value_in, key_in, query_in, cotangent, filter_param):
    groups = lax.axis_size("ctx")
    channels = filter_param.shape[0]
    extent = filter_param.shape[1]
    scale = 1.0 / math.sqrt(extent * groups)
    gated = (key_in * value_in)[0]
    taps = filter_param * scale
    weight_grad = (cotangent * query_in)[0]
    spec_real, spec_imag = forward_spectrum(jnp.concatenate([gated, taps], 0))
    gated_spec = (spec_real[:channels], spec_imag[:channels])
    taps_spec = (spec_real[channels:], spec_imag[channels:])
    conv = run_inverse([multiply_spectra(gated_spec, taps_spec, False)], channels)[0]
    weight_spec = forward_spectrum(weight_grad)
    gated_grad, filter_term = run_inverse(
        [
            multiply_spectra(weight_spec, taps_spec, True),
            multiply_spectra(weight_spec, gated_spec, True),
        ],
        channels,
    )
    filter_grad = lax.psum(filter_term, "dp") * scale
    query_grad = (cotangent[0] * conv)[None]
    key_grad = (gated_grad * value_in[0])[None]
    value_grad = (gated_grad * key_in[0])[None]
    return (query_grad, key_grad, value_grad, filter_grad)


def solution(mesh):
    return jax.shard_map(
        on_device,
        mesh=mesh,
        in_specs=(
            P("dp", None, "ctx"),
            P("dp", None, "ctx"),
            P("dp", None, "ctx"),
            P("dp", None, "ctx"),
            P(None, "ctx"),
        ),
        out_specs=(
            P("dp", None, "ctx"),
            P("dp", None, "ctx"),
            P("dp", None, "ctx"),
            P(None, "ctx"),
        ),
        check_vma=False,
    )
```

profile of v0, /device:TPU:2, one launch (start us, length us, event | category | flops | bytes accessed | tf_op | source)
XLA Modules:
  0.0 330.2 jit_solution(18212345920340852152)
XLA Ops:
  7.2 1.0 copy.240
  8.3 0.7 mul.1119
  9.0 6.3 %all-to-all-start.4 = ((f32[128,1,256]{0,1,2:T(1,128)}), f32[128,1,256]{0,1,2:T(1,128)S(1)}, u32[]{:S(2)}, u32[]{:S(2)}) async-start(f32[128,1,256]{0,1,2:T(1,128)} %bitcast.39), calls=%async_computation.4 | async-start | bytes 262144 | tf_op jit(solution)/shard_map/all_to_all | solution.py:50
  15.4 0.8 copy-done.5
  16.3 0.8 copy-done.6
  17.3 1.0 copy.214
  18.4 1.8 all-to-all-done.4
  20.2 5.3 %all-to-all-start = ((f32[256,1,256]{0,1,2:T(1,128)}), f32[256,1,256]{0,1,2:T(1,128)S(1)}, u32[]{:S(2)}, u32[]{:S(2)}) async-start(f32[256,1,256]{0,1,2:T(1,128)} %copy.214), calls=%async_computation | async-start | bytes 524288 | tf_op jit(solution)/shard_map/all_to_all | solution.py:50
  26.5 1.1 copy.245
  27.6 3.4 %all-to-all-done = f32[256,1,256]{0,1,2:T(1,128)S(1)} async-done(((f32[256,1,256]{0,1,2:T(1,128)}), f32[256,1,256]{0,1,2:T(1,128)S(1)}, u32[]{:S(2)}, u32[]{:S(2)}) %all-to-all-start) | async-done | bytes 262176 | tf_op jit(solution)/shard_map/all_to_all | solution.py:50
  31.0 6.1 %all-to-all-start.5 = ((f32[2,128,32,16]{1,3,0,2:T(8,128)}), f32[2,128,32,16]{1,3,0,2:T(8,128)S(1)}, u32[]{:S(2)}, u32[]{:S(2)}) async-start(f32[2,128,32,16]{1,3,0,2:T(8,128)} %copy.245), calls=%async_computation.5 | async-start | bytes 1048576 | tf_op jit(solution)/shard_map/all_to_all | solution.py:57
  37.3 0.7 fusion.4
  38.0 0.9 add_bitcast_fusion
  39.0 1.6 copy.217
  40.6 4.8 %all-to-all-done.5 = f32[2,128,32,16]{1,3,0,2:T(8,128)S(1)} async-done(((f32[2,128,32,16]{1,3,0,2:T(8,128)}), f32[2,128,32,16]{1,3,0,2:T(8,128)S(1)}, u32[]{:S(2)}, u32[]{:S(2)}) %all-to-all-start.5) | async-done | bytes 524320 | tf_op jit(solution)/shard_map/all_to_all | solution.py:57
  45.3 6.4 %all-to-all-start.1 = ((f32[2,256,32,16]{1,3,0,2:T(8,128)}), f32[2,256,32,16]{1,3,0,2:T(8,128)S(1)}, u32[]{:S(2)}, u32[]{:S(2)}) async-start(f32[2,256,32,16]{1,3,0,2:T(8,128)} %copy.217), calls=%async_computation.1 | async-start | bytes 2097152 | tf_op jit(solution)/shard_map/all_to_all | solution.py:57
  52.2 1.0 fusion.131
  53.3 1.0 fusion.145
  54.3 1.0 fusion.143
  55.4 1.0 fusion.133
  57.8 0.6 convolution_add_fusion.3
  58.4 7.1 %all-to-all-done.1 = f32[2,256,32,16]{1,3,0,2:T(8,128)S(1)} async-done(((f32[2,256,32,16]{1,3,0,2:T(8,128)}), f32[2,256,32,16]{1,3,0,2:T(8,128)S(1)}, u32[]{:S(2)}, u32[]{:S(2)}) %all-to-all-start.1) | async-done | bytes 1048608 | tf_op jit(solution)/shard_map/all_to_all | solution.py:57
  66.0 2.7 fusion.149
  69.1 1.9 fusion.151
  71.1 2.2 fusion.3
  73.3 2.4 multiply_add_fusion.2
  75.7 0.8 fusion.16
  76.5 0.8 fusion.12
  77.3 0.8 convolution_add_fusion.2
  78.2 0.8 convolution_subtract_fusion.2
  79.0 0.7 multiply_subtract_fusion.4
  79.8 0.8 fusion.20
  80.6 0.8 fusion.21
  81.4 0.8 fusion.18
  82.2 0.8 fusion.19
  83.7 1.0 fusion.53
  85.3 0.7 multiply_subtract_fusion.6
  86.0 1.1 fusion.30
  87.1 1.1 fusion.26
  88.2 1.1 fusion.8
  89.4 1.1 fusion.9
  91.3 1.0 copy.235
  92.3 6.5 %all-to-all-start.2 = ((f32[2,128,2,256]{1,2,0,3:T(2,128)}), f32[2,128,2,256]{1,2,0,3:T(2,128)S(1)}, u32[]{:S(2)}, u32[]{:S(2)}) async-start(f32[2,128,2,256]{1,2,0,3:T(2,128)} %copy.235), calls=%async_computation.2 | async-start | bytes 1048576 | tf_op jit(solution)/shard_map/all_to_all | solution.py:87
  98.8 1.4 multiply_subtract_fusion.1
  100.1 1.9 fusion.139
  102.1 2.0 fusion
  105.1 1.9 fusion.141
  107.0 2.0 fusion.1
  109.8 1.3 copy.263
  111.1 6.1 %all-to-all-start.6 = ((f32[2,256,2,256]{1,2,0,3:T(2,128)}), f32[2,256,2,256]{1,2,0,3:T(2,128)S(1)}, u32[]{:S(2)}, u32[]{:S(2)}) async-start(f32[2,256,2,256]{1,2,0,3:T(2,128)} %copy.263), calls=%async_computation.6 | async-start | bytes 2097152 | tf_op jit(solution)/shard_map/all_to_all | solution.py:87
  117.2 13.8 %all-to-all-done.6 = f32[2,256,2,256]{1,2,0,3:T(2,128)S(1)} async-done(((f32[2,256,2,256]{1,2,0,3:T(2,128)}), f32[2,256,2,256]{1,2,0,3:T(2,128)S(1)}, u32[]{:S(2)}, u32[]{:S(2)}) %all-to-all-start.6) | async-done | bytes 1048608 | tf_op jit(solution)/shard_map/all_to_all | solution.py:87
  133.8 0.9 copy.267
  134.7 6.1 %all-to-all-start.7 = ((f32[1,256,16,16]{1,3,0,2:T(8,128)}), f32[1,256,16,16]{1,3,0,2:T(8,128)S(1)}, u32[]{:S(2)}, u32[]{:S(2)}) async-start(f32[1,256,16,16]{1,3,0,2:T(8,128)} %copy.267), calls=%async_computation.7 | async-start | bytes 524288 | tf_op jit(solution)/shard_map/all_to_all | solution.py:97
  141.9 0.7 copy.239
  142.6 3.7 %all-to-all-done.7 = f32[1,256,16,16]{1,3,0,2:T(8,128)S(1)} async-done(((f32[1,256,16,16]{1,3,0,2:T(8,128)}), f32[1,256,16,16]{1,3,0,2:T(8,128)S(1)}, u32[]{:S(2)}, u32[]{:S(2)}) %all-to-all-start.7) | async-done | bytes 262176 | tf_op jit(solution)/shard_map/all_to_all | solution.py:97
  146.3 6.0 %all-to-all-start.3 = ((f32[1,128,16,16]{1,3,0,2:T(8,128)}), f32[1,128,16,16]{1,3,0,2:T(8,128)S(1)}, u32[]{:S(2)}, u32[]{:S(2)}) async-start(f32[1,128,16,16]{1,3,0,2:T(8,128)} %copy.239), calls=%async_computation.3 | async-start | bytes 262144 | tf_op jit(solution)/shard_map/all_to_all | solution.py:97
  152.4 0.7 slice_bitcast_fusion
  153.1 4.2 %all-to-all-done.3 = f32[1,128,16,16]{1,3,0,2:T(8,128)S(1)} async-done(((f32[1,128,16,16]{1,3,0,2:T(8,128)}), f32[1,128,16,16]{1,3,0,2:T(8,128)S(1)}, u32[]{:S(2)}, u32[]{:S(2)}) %all-to-all-start.3) | async-done | bytes 131104 | tf_op jit(solution)/shard_map/all_to_all | solution.py:97
  157.3 0.8 copy.270
  158.0 0.8 copy.272
  158.8 0.8 copy.271
  159.5 161.9 %all-reduce.2.cloned.1.call-done = f32[128,256]{0,1:T(8,128)} async-done(((f32[128,256]{0,1:T(8,128)}), f32[128,256]{0,1:T(8,128)}) %all-reduce.2.cloned.1.call-update) | async-done | bytes 131088 | tf_op jit(solution)/shard_map/psum | solution.py:140
  321.5 0.9 broadcast_multiply_fusion
  322.4 0.8 copy.273
  (72 shorter events, 12.2 us)
Async XLA Ops:
  7.2 1.0 copy-start.3
  9.0 6.3 %copy-start.4 = (f32[1,128,256]{2,1,0:T(8,128)S(1)}, f32[1,128,256]{2,1,0:T(8,128)}, u32[]{:S(2)}) copy-start(f32[1,128,256]{2,1,0:T(8,128)} %param.5) | copy-start | bytes 393220
  9.0 11.2 %all-to-all-start.4 = ((f32[128,1,256]{0,1,2:T(1,128)}), f32[128,1,256]{0,1,2:T(1,128)S(1)}, u32[]{:S(2)}, u32[]{:S(2)}) async-start(f32[128,1,256]{0,1,2:T(1,128)} %bitcast.39), calls=%async_computation.4 | async-start | bytes 262144 | tf_op jit(solution)/shard_map/all_to_all | solution.py:50
  15.3 0.9 copy-start.5
  16.2 0.9 copy-start.6
  20.2 10.8 %all-to-all-start = ((f32[256,1,256]{0,1,2:T(1,128)}), f32[256,1,256]{0,1,2:T(1,128)S(1)}, u32[]{:S(2)}, u32[]{:S(2)}) async-start(f32[256,1,256]{0,1,2:T(1,128)} %copy.214), calls=%async_computation | async-start | bytes 524288 | tf_op jit(solution)/shard_map/all_to_all | solution.py:50
  31.0 14.3 %all-to-all-start.5 = ((f32[2,128,32,16]{1,3,0,2:T(8,128)}), f32[2,128,32,16]{1,3,0,2:T(8,128)S(1)}, u32[]{:S(2)}, u32[]{:S(2)}) async-start(f32[2,128,32,16]{1,3,0,2:T(8,128)} %copy.245), calls=%async_computation.5 | async-start | bytes 1048576 | tf_op jit(solution)/shard_map/all_to_all | solution.py:57
  45.3 20.2 %all-to-all-start.1 = ((f32[2,256,32,16]{1,3,0,2:T(8,128)}), f32[2,256,32,16]{1,3,0,2:T(8,128)S(1)}, u32[]{:S(2)}, u32[]{:S(2)}) async-start(f32[2,256,32,16]{1,3,0,2:T(8,128)} %copy.217), calls=%async_computation.1 | async-start | bytes 2097152 | tf_op jit(solution)/shard_map/all_to_all | solution.py:57
  71.1 2.2 copy-start.2
  92.3 18.9 %all-to-all-start.2 = ((f32[2,128,2,256]{1,2,0,3:T(2,128)}), f32[2,128,2,256]{1,2,0,3:T(2,128)S(1)}, u32[]{:S(2)}, u32[]{:S(2)}) async-start(f32[2,128,2,256]{1,2,0,3:T(2,128)} %copy.235), calls=%async_computation.2 | async-start | bytes 1048576 | tf_op jit(solution)/shard_map/all_to_all | solution.py:87
  100.1 1.9 copy-start
  104.1 1.0 copy-start.1
  111.1 19.9 %all-to-all-start.6 = ((f32[2,256,2,256]{1,2,0,3:T(2,128)}), f32[2,256,2,256]{1,2,0,3:T(2,128)S(1)}, u32[]{:S(2)}, u32[]{:S(2)}) async-start(f32[2,256,2,256]{1,2,0,3:T(2,128)} %copy.263), calls=%async_computation.6 | async-start | bytes 2097152 | tf_op jit(solution)/shard_map/all_to_all | solution.py:87
  134.7 11.6 %all-to-all-start.7 = ((f32[1,256,16,16]{1,3,0,2:T(8,128)}), f32[1,256,16,16]{1,3,0,2:T(8,128)S(1)}, u32[]{:S(2)}, u32[]{:S(2)}) async-start(f32[1,256,16,16]{1,3,0,2:T(8,128)} %copy.267), calls=%async_computation.7 | async-start | bytes 524288 | tf_op jit(solution)/shard_map/all_to_all | solution.py:97
  146.3 10.9 %all-to-all-start.3 = ((f32[1,128,16,16]{1,3,0,2:T(8,128)}), f32[1,128,16,16]{1,3,0,2:T(8,128)S(1)}, u32[]{:S(2)}, u32[]{:S(2)}) async-start(f32[1,128,16,16]{1,3,0,2:T(8,128)} %copy.239), calls=%async_computation.3 | async-start | bytes 262144 | tf_op jit(solution)/shard_map/all_to_all | solution.py:97
  152.3 169.1 %all-reduce.2.cloned.1.call-start = ((), (), s32[]{:S(2)}) async-start(), calls=%async_computation.8 | async-start | bytes 262144 | tf_op jit(solution)/shard_map/psum | solution.py:140
Sparse Core Ops, SparseCore 0:
  155.8 165.6 all-reduce.1
where the time goes:
time: 335 us; the launch traced here: 330 us
  waiting for transfers between devices  201 us (60%)
  starting transfers between devices  48.7 us (15%)
  matrix products  41.9 us (13%)
  local copies, waits for them, and re-layouts  19.5 us (6%)
  between operations  15 us (4%)
  other arithmetic  4.54 us (1%)
    psum x1, waiting for transfers between devices, on_device(): filter_grad = lax.psum(filter_term, 'dp') * scale  162 us
    dot_general x32, matrix products, contract(): return jnp.einsum(formula, table, values, precision=exact_mode)  37.8 us
    all_to_all x2, waiting for transfers between devices, inverse_signal(): lax.all_to_all(jnp.stack([real_part, imag_part]), 'ctx', split_axis=3, co...  13.8 us
    all_to_all x2, starting transfers between devices, inverse_signal(): lax.all_to_all(jnp.stack([real_part, imag_part]), 'ctx', split_axis=3, co...  12.5 us
    all_to_all x2, starting transfers between devices, forward_spectrum(): lax.all_to_all(jnp.stack([real_part, imag_part]), 'ctx', split_axis=2, co...  12.4 us
    all_to_all x2, starting transfers between devices, inverse_signal(): lax.all_to_all(stacked, 'ctx', split_axis=2, concat_axis=3, tiled=True)  12.1 us
    all_to_all x2, waiting for transfers between devices, forward_spectrum(): lax.all_to_all(jnp.stack([real_part, imag_part]), 'ctx', split_axis=2, co...  11.9 us
    all_to_all x2, starting transfers between devices, forward_spectrum(): lax.all_to_all(signal[:, None, :], 'ctx', split_axis=2, concat_axis=1, ti...  11.6 us
  transfers between devices with their start and end apart: 9, of which 8 were waited for; matrix products, arithmetic and copies ran while one was open for 9% of the time, Pallas kernels for 0%

commit v1 on v0

v1 whole, which is shorter than its diff:
```python
import math

import jax
import jax.numpy as jnp
import numpy as np
from jax import lax
from jax.experimental import pallas as pl
from jax.experimental.pallas import tpu as pltpu
from jax.sharding import Mesh, PartitionSpec as P

AXES = ("zh", "y", "x", "zl", "core")
FAR = ("y", "x", "zl", "core")
BLOCKS = 17
CLASSES = [0, 16, 8, 4, 20] + [8 * j + 2 for j in range(4)] + [4 * j + 1 for j in range(8)]
VMEM = pl.BlockSpec(memory_space=pltpu.VMEM)
HBM = pl.BlockSpec(memory_space=pltpu.HBM)
PARAMS = pltpu.CompilerParams(vmem_limit_bytes=48 * 1024 * 1024)


def tables():
    lane = np.arange(128)
    forward = np.zeros((256, 256))
    angle = 2 * np.pi * np.outer(lane, lane) / 128
    c, s = np.cos(angle), np.sin(angle)
    forward = np.block([[c, -s], [s, c]])
    inverse = np.block([[c, s], [-s, c]]) * (2.0 / 8192)

    def split(table):
        high = table.astype(np.float32).astype(jnp.bfloat16)
        low = (table - high.astype(np.float64)).astype(np.float32).astype(jnp.bfloat16)
        return np.concatenate([high, low], 0)

    row_half = np.arange(8) // 4
    twiddle = np.zeros((BLOCKS, 2, 8, 128), np.float32)
    rowfix = np.zeros((BLOCKS, 2, 8, 128), np.float32)
    for index, k in enumerate(CLASSES):
        angle = -2 * np.pi * np.outer(k + 32 * row_half, lane) / 8192
        twiddle[index, 0], twiddle[index, 1] = np.cos(angle), np.sin(angle)
        angle = np.repeat((-2 * np.pi * k * row_half / 64)[:, None], 128, 1)
        rowfix[index, 0], rowfix[index, 1] = np.cos(angle), np.sin(angle)
    return split(forward), split(inverse), twiddle, rowfix


def add(a, b):
    return (a[0] + b[0], a[1] + b[1])


def sub(a, b):
    return (a[0] - b[0], a[1] - b[1])


def turn(a, step, period, sign):
    step = step % period
    if step == 0:
        return a
    if 4 * step == period:
        return (-a[1], a[0]) if sign > 0 else (a[1], -a[0])
    if 8 * step == period:
        r = np.float32(math.sqrt(0.5))
        if sign > 0:
            return ((a[0] - a[1]) * r, (a[0] + a[1]) * r)
        return ((a[0] + a[1]) * r, (a[1] - a[0]) * r)
    angle = sign * 2 * math.pi * step / period
    c, s = np.float32(math.cos(angle)), np.float32(math.sin(angle))
    return (a[0] * c - a[1] * s, a[0] * s + a[1] * c)


def small_dft(z, sign):
    n = len(z)
    if n == 1:
        return z
    even, odd = small_dft(z[0::2], sign), small_dft(z[1::2], sign)
    odd = [turn(value, j, n, sign) for j, value in enumerate(odd)]
    return [add(a, b) for a, b in zip(even, odd)] + [sub(a, b) for a, b in zip(even, odd)]


def blocks_forward(x):
    v = [x[c] + x[c + 8] for c in range(8)]
    u = [x[c] - x[c + 8] for c in range(8)]
    odd = small_dft([turn((x[c], -x[c + 8]), c, 32, -1) for c in range(8)], -1)
    two = small_dft([turn((u[c], -u[c + 4]), c, 16, -1) for c in range(4)], -1)
    a = [v[c] + v[c + 4] for c in range(4)]
    b = [v[c] - v[c + 4] for c in range(4)]
    four = small_dft([turn((b[c], -b[c + 2]), c, 8, -1) for c in range(2)], -1)
    e, o = a[0] + a[2], a[1] + a[3]
    eight = (a[0] - a[2], a[3] - a[1])
    return [(e + o, None), (e - o, None), eight] + four + two + odd


def blocks_inverse(spectrum):
    zero, sixteen, eight = spectrum[0], spectrum[1], spectrum[2]
    four, two, odd = spectrum[3:5], spectrum[5:9], spectrum[9:17]
    e, o = (zero[0] + sixteen[0]) * 0.5, (zero[0] - sixteen[0]) * 0.5
    a = [e + eight[0], o - eight[1], e - eight[0], o + eight[1]]
    g = [turn(value, c, 8, 1) for c, value in enumerate(small_dft(four, 1))]
    b = [g[0][0], g[1][0], -g[0][1], -g[1][1]]
    v = [a[c] + b[c] for c in range(4)] + [a[c] - b[c] for c in range(4)]
    g = [turn(value, c, 16, 1) for c, value in enumerate(small_dft(two, 1))]
    u = [value[0] for value in g] + [-value[1] for value in g]
    g = [turn(value, c, 32, 1) for c, value in enumerate(small_dft(odd, 1))]
    p = [v[c] + u[c] for c in range(8)]
    m = [v[c] - u[c] for c in range(8)]
    return [p[c] + g[c][0] for c in range(8)] + [m[c] - g[c][1] for c in range(8)]


def half_sign():
    rows = lax.broadcasted_iota(jnp.int32, (8, 128), 0)
    return jnp.where(rows < 4, 1.0, -1.0).astype(jnp.float32)


def swap_halves(a):
    return pltpu.roll(a, 4, 0)


def times(a, b, conjugate=False):
    if conjugate:
        return (a[0] * b[0] + a[1] * b[1], a[1] * b[0] - a[0] * b[1])
    return (a[0] * b[0] - a[1] * b[1], a[0] * b[1] + a[1] * b[0])


def butterfly(a, sign):
    return (a[0] * sign + swap_halves(a[0]), a[1] * sign + swap_halves(a[1]))


def multiply(source, target, table, rows, step):
    high_table, low_table = table[0:256, :], table[256:512, :]
    for start in range(0, rows, step):
        block = source[start : start + step, :]
        high = block.astype(jnp.bfloat16)
        low = (block - high.astype(jnp.float32)).astype(jnp.bfloat16)
        total = jnp.dot(high, low_table, preferred_element_type=jnp.float32)
        total += jnp.dot(low, high_table, preferred_element_type=jnp.float32)
        total += jnp.dot(high, high_table, preferred_element_type=jnp.float32)
        target[start : start + step, :] = total


def pack_kernel(value_hbm, key_hbm, query_hbm, cot_hbm, filter_hbm, out_ref, value_ref, key_ref, query_ref, cot_ref, filter_ref, sems):
    copies = [
        pltpu.make_async_copy(value_hbm, value_ref, sems.at[0]),
        pltpu.make_async_copy(key_hbm, key_ref, sems.at[1]),
        pltpu.make_async_copy(cot_hbm, cot_ref, sems.at[2]),
        pltpu.make_async_copy(query_hbm, query_ref, sems.at[3]),
        pltpu.make_async_copy(filter_hbm, filter_ref, sems.at[4]),
    ]
    for copy in copies:
        copy.start()
    y = lax.axis_index("y")
    tap_half, tap_channel = y // 2, y % 2
    tap_lanes = pl.ds(pl.multiple_of(tap_half * 128, 128), 128)
    tap_rows = pl.ds(pl.multiple_of(tap_channel * 64, 64), 64)
    places = [(half * 4 + j, pl.ds(j * 64, 64), pl.ds(half * 128, 128)) for j in range(2) for half in range(2)]
    copies[0].wait()
    copies[1].wait()
    for at, rows, lanes in places:
        out_ref[pl.ds(at, 64, stride=9), :] = key_ref[rows, lanes] * value_ref[rows, lanes]
    copies[2].wait()
    copies[3].wait()
    for at, rows, lanes in places:
        out_ref[pl.ds(at + 2, 64, stride=9), :] = cot_ref[rows, lanes] * query_ref[rows, lanes]
    copies[4].wait()
    out_ref[pl.ds(8, 64, stride=9), :] = filter_ref[tap_rows, tap_lanes] * (1.0 / 64)


def spectrum_rows(blocks, scratch, base, stride, sign, twiddle_ref, rowfix_ref):
    for index, value in enumerate(blocks_forward(blocks)):
        fix = (rowfix_ref[index, 0], rowfix_ref[index, 1])
        if value[1] is None:
            value = (value[0] * fix[0], value[0] * fix[1])
        else:
            value = times(value, fix)
        value = butterfly(value, sign)
        value = times(value, (twiddle_ref[index, 0], twiddle_ref[index, 1]))
        at = base + index * stride
        scratch[at : at + 8, 0:128] = value[0]
        scratch[at : at + 8, 128:256] = value[1]


def blocks_of(scratch, base, stride, sign, twiddle_ref, rowfix_ref):
    spectrum = []
    for index in range(BLOCKS):
        at = base + index * stride
        value = (scratch[at : at + 8, 0:128], scratch[at : at + 8, 128:256])
        value = times(value, (twiddle_ref[index, 0], twiddle_ref[index, 1]), True)
        value = butterfly(value, sign)
        spectrum.append(times(value, (rowfix_ref[index, 0], rowfix_ref[index, 1]), True))
    return blocks_inverse(spectrum)


def forward_kernel(signal_ref, forward_ref, inverse_ref, twiddle_ref, rowfix_ref, spec_ref, part_ref, raw, spec, taps):
    sign = half_sign()
    for y in range(4):
        at = (y // 2) * 4 + y % 2
        for c in range(0, 16, 8):
            rows = signal_ref[pl.ds((y * 16 + c) * 9 + 8, 8, stride=9), :]
            taps[pl.ds(c * 8 + at, 8, stride=8), :] = rows
            taps[pl.ds(c * 8 + at + 2, 8, stride=8), :] = rows
    spectrum_rows([taps[c * 8 : c * 8 + 8, :] for c in range(16)], raw, 544, 8, sign, twiddle_ref, rowfix_ref)
    for y in range(4):
        blocks = [signal_ref[(y * 16 + c) * 9 : (y * 16 + c) * 9 + 8, :] for c in range(16)]
        spectrum_rows(blocks, raw, y * 8, 32, sign, twiddle_ref, rowfix_ref)
    multiply(raw, spec, forward_ref, 680, 136)
    rows = lax.broadcasted_iota(jnp.int32, (8, 128), 0)
    flip = jnp.where(rows % 4 < 2, 1.0, -1.0).astype(jnp.float32)
    for index in range(BLOCKS):
        at = 544 + index * 8
        tap = (spec[at : at + 8, 0:128], spec[at : at + 8, 128:256] * flip)
        total = None
        for y in range(4):
            at = index * 32 + y * 8
            value = (spec[at : at + 8, 0:128], spec[at : at + 8, 128:256])
            product = times(value, tap)
            spec_ref[at : at + 8, 0:128] = product[0]
            spec_ref[at : at + 8, 128:256] = product[1]
            weight = (pltpu.roll(value[0], 6, 0), pltpu.roll(value[1], 6, 0))
            term = times(weight, value, True)
            total = term if total is None else add(total, term)
        raw[index * 8 : index * 8 + 8, 0:128] = total[0]
        raw[index * 8 : index * 8 + 8, 128:256] = total[1]
    multiply(raw, spec, inverse_ref, 136, 136)
    blocks = blocks_of(spec, 0, 8, sign, twiddle_ref, rowfix_ref)
    for c in range(16):
        for half in range(2):
            rows2 = blocks[c][half * 4 : half * 4 + 2, :]
            for copy in range(4):
                at = copy * 64 + c * 4 + half * 2
                part_ref[at : at + 2, :] = rows2


def inverse_kernel(spec_ref, inverse_ref, twiddle_ref, rowfix_ref, out_ref, raw):
    sign = half_sign()
    multiply(spec_ref, raw, inverse_ref, 544, 136)
    for y in range(4):
        blocks = blocks_of(raw, y * 8, 32, sign, twiddle_ref, rowfix_ref)
        for c in range(16):
            at = (y * 16 + c) * 12
            out_ref[at : at + 8, :] = blocks[c]


def filter_kernel(part_ref, message_ref, out_ref):
    out_ref[...] = message_ref[...]
    for c in range(0, 16, 2):
        pair = part_ref[c * 4 : c * 4 + 8, :]
        for copy in range(1, 4):
            pair = pair + part_ref[copy * 64 + c * 4 : copy * 64 + c * 4 + 8, :]
        pair = pair * (1.0 / 64)
        for y in range(4):
            at = (y * 16 + c) * 12
            out_ref[at + 8 : at + 12, :] = pair[0:4, :]
            out_ref[at + 20 : at + 24, :] = pair[4:8, :]


def unpack_kernel(signal_ref, value_ref, key_ref, cot_ref, query_out, key_out, value_out, filter_out):
    for j in range(2):
        rows = pl.ds(j * 64, 64)
        for half in range(2):
            lanes = pl.ds(half * 128, 128)
            at = half * 4 + j
            conv = signal_ref[pl.ds(at, 64, stride=12), :]
            grad = signal_ref[pl.ds(at + 2, 64, stride=12), :]
            query_out[rows, lanes] = cot_ref[rows, lanes] * conv
            key_out[rows, lanes] = grad * value_ref[rows, lanes]
            value_out[rows, lanes] = grad * key_ref[rows, lanes]
            filter_out[rows, lanes] = signal_ref[pl.ds(8 + half * 2 + j, 64, stride=12), :]


def call(kernel, shapes, inputs, scratch=(), copies=0, **extra):
    return pl.pallas_call(
        kernel,
        out_shape=[jax.ShapeDtypeStruct(shape, jnp.float32) for shape in shapes],
        in_specs=[HBM if copies else VMEM] * inputs,
        out_specs=[VMEM] * len(shapes),
        scratch_shapes=[pltpu.VMEM(shape, jnp.float32) for shape in scratch]
        + ([pltpu.SemaphoreType.DMA((copies,))] if copies else []),
        compiler_params=PARAMS,
        **extra,
    )


def exchange(array, axes):
    return lax.all_to_all(array, axes, split_axis=0, concat_axis=0, tiled=True)


def on_device(value_in, key_in, query_in, cotangent, filter_param):
    value_in, key_in, query_in, cotangent = value_in[0], key_in[0], query_in[0], cotangent[0]
    forward, inverse, twiddle, rowfix = [jnp.asarray(table) for table in tables()]
    pinned = [pltpu.with_memory_space_constraint(a, pltpu.HBM) for a in (value_in, key_in, query_in, cotangent, filter_param)]
    (message,) = call(pack_kernel, [(576, 128)], 5, [(128, 256)] * 5, copies=5)(
        *pinned
    )
    signal = exchange(message.reshape(64, 1, 1152), FAR).reshape(576, 128)
    spec, part = call(forward_kernel, [(544, 256), (256, 128)], 5, [(680, 256), (680, 256), (128, 128)])(
        signal, forward, inverse, twiddle, rowfix
    )
    (message,) = call(inverse_kernel, [(768, 128)], 4, [(544, 256)])(spec, inverse, twiddle, rowfix)
    part, message = lax.optimization_barrier((part, message))
    parts = exchange(part.reshape(4, 64, 128), ("zh",)).reshape(256, 128)
    (message,) = call(filter_kernel, [(768, 128)], 2)(parts, message)
    signal = exchange(message.reshape(64, 1, 1536), FAR).reshape(768, 128)
    shape = (128, 256)
    query_grad, key_grad, value_grad, filter_grad = call(unpack_kernel, [shape] * 4, 4)(
        signal, value_in, key_in, cotangent
    )
    return query_grad[None], key_grad[None], value_grad[None], filter_grad


def solution(mesh):
    fine = Mesh(mesh.devices.reshape(4, 4, 4, 2, 2), AXES)
    signal = P(("zh", "y"), None, ("x", "zl", "core"))
    taps = P(None, ("x", "zl", "core"))
    return jax.shard_map(
        on_device,
        mesh=fine,
        in_specs=(signal, signal, signal, signal, taps),
        out_specs=(signal, signal, signal, taps),
        check_vma=False,
    )
```

time: 335 us -> 57.3 us (0.17)
  the two profiles are of different devices: /device:TPU:2 before, /device:TPU:1 now
where the time goes in v1:
time: 57.3 us; the launch traced here: 57.1 us
  blocking collectives  52.8 us (92%)
  Pallas kernels  3.51 us (6%)
  between operations  0.73 us (1%)
    all_to_all x3, blocking collectives, exchange(): return lax.all_to_all(array, axes, split_axis=0, concat_axis=0, tiled=True)  52.8 us
    pallas_call x1, Pallas kernels, on_device(): call(pack_kernel, [(576, 128)], 5, [(128, 256)] * 5, copies=5)(*pinned)  1.25 us

profile of v1, /device:TPU:1, one launch (start us, length us, event | category | flops | bytes accessed | tf_op | source)
XLA Modules:
  0.0 57.1 jit_solution(14736677202668792660)
XLA Ops:
  0.6 0.0 copy-start.6
  0.6 1.2 %shard_map.120 = f32[576,128]{1,0:T(8,128)S(1)} custom-call(f32[128,256]{1,0:T(8,128)} %bitcast.18, f32[128,256]{1,0:T(8,128)} %bitcast.20, f32[128,256]{1,0:T(8,128)} %bitcast.25, f32[128,256]{1,0:T(8,128)} %bitcast.22, f32[128,256]{1,0:T(8,128)} %filter_hbm.1), custom_call_target="tpu_custom_call" | custom-call | tf_op jit(solution)/shard_map/pallas_call | solution.py:287
  1.9 0.0 copy-start
  1.9 0.0 copy-start.1
  1.9 0.0 copy-start.2
  1.9 20.6 %all_to_all.15 = f32[64,1,1152]{2,1,0:T(1,128)S(1)} all-to-all(f32[64,1,1152]{2,1,0:T(1,128)S(1)} %bitcast.16), channel_id=1, replica_groups=mesh['zh'=4,'y'=4,'x'=4,'zl'=2,'core'=2] {'y','x','zl','core'}, dimensions={0} | all-to-all | bytes 589824 | tf_op jit(solution)/shard_map/all_to_all | solution.py:280
  22.6 0.0 copy-done.6
  22.6 0.0 copy-done
  22.6 0.0 copy-done.1
  22.6 0.0 copy-done.2
  22.6 0.9 %shard_map.121 = (f32[544,256]{1,0:T(8,128)S(1)}, f32[256,128]{1,0:T(8,128)S(1)}) custom-call(f32[576,128]{1,0:T(8,128)S(1)} %bitcast.15, bf16[512,256]{1,0:T(8,128)(2,1)S(1)} %copy-done.6, bf16[512,256]{1,0:T(8,128)(2,1)S(1)} %copy-done, f32[17,2,8,128]{3,2,1,0:T(8,128)S(1)} %copy-done.2, f32[17,2,8,128]{3,2,1,0:T(8,128)S(1)} %copy-done.1), custom_call_target="tpu_custom_call" | custom-call | tf_op jit(solution)/shard_map/pallas_call | solution.py:291
  23.4 0.5 shard_map.122.message_ref
  24.0 14.4 %all_to_all.16 = f32[4,64,128]{2,1,0:T(8,128)S(1)} all-to-all(f32[4,64,128]{2,1,0:T(8,128)S(1)} %bitcast.24), channel_id=1, replica_groups=mesh['zh'=4,'y'=4,'x'=4,'zl'=2,'core'=2] {'zh'}, dimensions={0} | all-to-all | bytes 262144 | tf_op jit(solution)/shard_map/all_to_all | solution.py:280
  38.4 0.0 copy-start.3
  38.4 0.0 copy-start.4
  38.4 0.0 copy-start.5
  38.4 17.8 %all_to_all.17 = f32[64,1,1536]{2,1,0:T(1,128)S(1)} all-to-all(f32[64,1,1536]{2,1,0:T(1,128)S(1)} %bitcast.14), channel_id=1, replica_groups=mesh['zh'=4,'y'=4,'x'=4,'zl'=2,'core'=2] {'y','x','zl','core'}, dimensions={0} | all-to-all | bytes 786432 | tf_op jit(solution)/shard_map/all_to_all | solution.py:280
  56.2 0.0 copy-done.3
  56.2 0.0 copy-done.4
  56.2 0.0 copy-done.5
  56.2 0.8 %shard_map.124 = (f32[128,256]{1,0:T(8,128)}, f32[128,256]{1,0:T(8,128)}, f32[128,256]{1,0:T(8,128)}, f32[128,256]{1,0:T(8,128)}) custom-call(f32[768,128]{1,0:T(8,128)S(1)} %bitcast.13, f32[128,256]{1,0:T(8,128)S(1)} %bitcast.19, f32[128,256]{1,0:T(8,128)S(1)} %bitcast.21, f32[128,256]{1,0:T(8,128)S(1)} %bitcast.23), custom_call_target="tpu_custom_call" | custom-call | tf_op jit(solution)/shard_map/pallas_call | solution.py:300
  (1 shorter events, 0.0 us)
Async XLA Ops:
  0.6 21.9 %copy-start.6 = (bf16[512,256]{1,0:T(8,128)(2,1)S(1)}, bf16[512,256]{1,0:T(8,128)(2,1)}, u32[]{:S(2)}) copy-start(bf16[512,256]{1,0:T(8,128)(2,1)} %constant.8.clone.forward_ref) | copy-start | bytes 786436
  1.9 20.7 %copy-start = (bf16[512,256]{1,0:T(8,128)(2,1)S(1)}, bf16[512,256]{1,0:T(8,128)(2,1)}, u32[]{:S(2)}) copy-start(bf16[512,256]{1,0:T(8,128)(2,1)} %constant.9.clone.inverse_ref) | copy-start | bytes 786436
  1.9 20.6 %copy-start.1 = (f32[17,2,8,128]{3,2,1,0:T(8,128)S(1)}, f32[17,2,8,128]{3,2,1,0:T(8,128)}, u32[]{:S(2)}) copy-start(f32[17,2,8,128]{3,2,1,0:T(8,128)} %constant.11.clone.rowfix_ref) | copy-start | bytes 417796
  1.9 20.6 %copy-start.2 = (f32[17,2,8,128]{3,2,1,0:T(8,128)S(1)}, f32[17,2,8,128]{3,2,1,0:T(8,128)}, u32[]{:S(2)}) copy-start(f32[17,2,8,128]{3,2,1,0:T(8,128)} %constant.10.clone.twiddle_ref) | copy-start | bytes 417796
  38.4 17.8 %copy-start.3 = (f32[1,128,256]{2,1,0:T(8,128)S(1)}, f32[1,128,256]{2,1,0:T(8,128)}, u32[]{:S(2)}) copy-start(f32[1,128,256]{2,1,0:T(8,128)} %param.9) | copy-start | bytes 393220
  38.4 17.8 %copy-start.4 = (f32[1,128,256]{2,1,0:T(8,128)S(1)}, f32[1,128,256]{2,1,0:T(8,128)}, u32[]{:S(2)}) copy-start(f32[1,128,256]{2,1,0:T(8,128)} %param.10) | copy-start | bytes 393220
  38.4 17.8 %copy-start.5 = (f32[1,128,256]{2,1,0:T(8,128)S(1)}, f32[1,128,256]{2,1,0:T(8,128)}, u32[]{:S(2)}) copy-start(f32[1,128,256]{2,1,0:T(8,128)} %param.12) | copy-start | bytes 393220

commit v2 on v1

--- a/solution.py
+++ b/solution.py
@@ -9,6 +9,7 @@
 from jax.sharding import Mesh, PartitionSpec as P
 
 AXES = ("zh", "y", "x", "zl", "core")
+STEPS = [[(0, 1), (1, 0), (2, 3), (3, 2)], [(0, 3), (3, 0), (1, 2), (2, 1)]]
 FAR = ("y", "x", "zl", "core")
 BLOCKS = 17
 CLASSES = [0, 16, 8, 4, 20] + [8 * j + 2 for j in range(4)] + [4 * j + 1 for j in range(8)]
@@ -221,9 +222,8 @@
     for c in range(16):
         for half in range(2):
             rows2 = blocks[c][half * 4 : half * 4 + 2, :]
-            for copy in range(4):
-                at = copy * 64 + c * 4 + half * 2
-                part_ref[at : at + 2, :] = rows2
+            at = c * 4 + half * 2
+            part_ref[at : at + 2, :] = rows2
 
 
 def inverse_kernel(spec_ref, inverse_ref, twiddle_ref, rowfix_ref, out_ref, raw):
@@ -236,12 +236,13 @@
             out_ref[at : at + 8, :] = blocks[c]
 
 
-def filter_kernel(part_ref, message_ref, out_ref):
+def filter_kernel(part_ref, *refs):
+    *more_refs, message_ref, out_ref = refs
     out_ref[...] = message_ref[...]
     for c in range(0, 16, 2):
         pair = part_ref[c * 4 : c * 4 + 8, :]
-        for copy in range(1, 4):
-            pair = pair + part_ref[copy * 64 + c * 4 : copy * 64 + c * 4 + 8, :]
+        for more in more_refs:
+            pair = pair + more[c * 4 : c * 4 + 8, :]
         pair = pair * (1.0 / 64)
         for y in range(4):
             at = (y * 16 + c) * 12
@@ -288,13 +289,14 @@
         *pinned
     )
     signal = exchange(message.reshape(64, 1, 1152), FAR).reshape(576, 128)
-    spec, part = call(forward_kernel, [(544, 256), (256, 128)], 5, [(680, 256), (680, 256), (128, 128)])(
+    spec, part = call(forward_kernel, [(544, 256), (64, 128)], 5, [(680, 256), (680, 256), (128, 128)])(
         signal, forward, inverse, twiddle, rowfix
     )
     (message,) = call(inverse_kernel, [(768, 128)], 4, [(544, 256)])(spec, inverse, twiddle, rowfix)
-    part, message = lax.optimization_barrier((part, message))
-    parts = exchange(part.reshape(4, 64, 128), ("zh",)).reshape(256, 128)
-    (message,) = call(filter_kernel, [(768, 128)], 2)(parts, message)
+    for pairs in STEPS:
+        part = part + lax.ppermute(part, "zh", pairs)
+    parts = [part]
+    (message,) = call(filter_kernel, [(768, 128)], 2)(*parts, message)
     signal = exchange(message.reshape(64, 1, 1536), FAR).reshape(768, 128)
     shape = (128, 256)
     query_grad, key_grad, value_grad, filter_grad = call(unpack_kernel, [shape] * 4, 4)(

time: 57.3 us -> 52.6 us (0.918)
  blocking collectives: 52.8 us -> 38.4 us
  starting transfers between devices: 0 us -> 7.65 us
  waiting for transfers between devices: 0 us -> 2.07 us
    all_to_all x3 -> x2, blocking collectives: 52.8 us -> 38.4 us  [exchange(): return lax.all_to_all(array, axes, split_axis=0, concat_axis=0, tiled=True)]
    ppermute x0 -> x2, starting transfers between devices: none -> 7.65 us  [on_device(): part = part + lax.ppermute(part, 'zh', pairs)]
    ppermute x0 -> x2, waiting for transfers between devices: none -> 2.07 us  [on_device(): part = part + lax.ppermute(part, 'zh', pairs)]
  transfers between devices with their start and end apart: 0 -> 2, of which waited for: 0 -> 2; matrix products, arithmetic and copies ran while one was open for 0% -> 0% of each run, Pallas kernels for 0% -> 1%
where the time goes in v2:
time: 52.6 us; the launch traced here: 52.4 us
  blocking collectives  38.4 us (73%)
  starting transfers between devices  7.65 us (15%)
  Pallas kernels  3.48 us (7%)
  waiting for transfers between devices  2.07 us (4%)
  between operations  0.73 us (1%)
    all_to_all x2, blocking collectives, exchange(): return lax.all_to_all(array, axes, split_axis=0, concat_axis=0, tiled=True)  38.4 us
    ppermute x2, starting transfers between devices, on_device(): part = part + lax.ppermute(part, 'zh', pairs)  7.65 us
    ppermute x2, waiting for transfers between devices, on_device(): part = part + lax.ppermute(part, 'zh', pairs)  2.07 us
    pallas_call x1, Pallas kernels, on_device(): call(pack_kernel, [(576, 128)], 5, [(128, 256)] * 5, copies=5)(*pinned)  1.25 us
  transfers between devices with their start and end apart: 2, of which 2 were waited for; matrix products, arithmetic and copies ran while one was open for 0% of the time, Pallas kernels for 1%

profile of v2, /device:TPU:1, one launch (start us, length us, event | category | flops | bytes accessed | tf_op | source)
XLA Modules:
  0.0 52.4 jit_solution(3862653809926856352)
XLA Ops:
  0.6 0.0 copy-start.6
  0.6 1.2 %shard_map.120 = f32[576,128]{1,0:T(8,128)S(1)} custom-call(f32[128,256]{1,0:T(8,128)} %bitcast.15, f32[128,256]{1,0:T(8,128)} %bitcast.17, f32[128,256]{1,0:T(8,128)} %bitcast.21, f32[128,256]{1,0:T(8,128)} %bitcast.19, f32[128,256]{1,0:T(8,128)} %filter_hbm.1), custom_call_target="tpu_custom_call" | custom-call | tf_op jit(solution)/shard_map/pallas_call | solution.py:288
  1.9 0.0 copy-start
  1.9 0.0 copy-start.1
  1.9 0.0 copy-start.2
  1.9 20.6 %all_to_all.10 = f32[64,1,1152]{2,1,0:T(1,128)S(1)} all-to-all(f32[64,1,1152]{2,1,0:T(1,128)S(1)} %bitcast.14), channel_id=1, replica_groups=mesh['zh'=4,'y'=4,'x'=4,'zl'=2,'core'=2] {'y','x','zl','core'}, dimensions={0} | all-to-all | bytes 589824 | tf_op jit(solution)/shard_map/all_to_all | solution.py:281
  22.6 0.0 copy-done.6
  22.6 0.0 copy-done
  22.6 0.0 copy-done.1
  22.6 0.0 copy-done.2
  22.6 0.8 %shard_map.121 = (f32[544,256]{1,0:T(8,128)S(1)}, f32[64,128]{1,0:T(8,128)S(1)}) custom-call(f32[576,128]{1,0:T(8,128)S(1)} %bitcast.13, bf16[512,256]{1,0:T(8,128)(2,1)S(1)} %copy-done.6, bf16[512,256]{1,0:T(8,128)(2,1)S(1)} %copy-done, f32[17,2,8,128]{3,2,1,0:T(8,128)S(1)} %copy-done.2, f32[17,2,8,128]{3,2,1,0:T(8,128)S(1)} %copy-done.1), custom_call_target="tpu_custom_call" | custom-call | tf_op jit(solution)/shard_map/pallas_call | solution.py:292
  23.4 3.1 %collective-permute-start = (f32[64,128]{1,0:T(8,128)S(1)}, f32[64,128]{1,0:T(8,128)S(1)}, u32[]{:S(2)}, u32[]{:S(2)}) collective-permute-start(f32[64,128]{1,0:T(8,128)S(1)} %get-tuple-element.10), channel_id=1, source_target_pairs={{0,64},{64,0},{128,192},{192,128},{1,65},{65,1},{129,193},{193,129... | collective-permute-start | bytes 98312 | tf_op jit(solution)/shard_map/ppermute | solution.py:297
  26.5 1.3 %collective-permute-done = f32[64,128]{1,0:T(8,128)S(1)} collective-permute-done((f32[64,128]{1,0:T(8,128)S(1)}, f32[64,128]{1,0:T(8,128)S(1)}, u32[]{:S(2)}, u32[]{:S(2)}) %collective-permute-start) | collective-permute-done | bytes 32800 | tf_op jit(solution)/shard_map/ppermute | solution.py:297
  27.8 4.6 %collective-permute-start.1 = (f32[64,128]{1,0:T(8,128)S(1)}, f32[64,128]{1,0:T(8,128)S(1)}, u32[]{:S(2)}, u32[]{:S(2)}) collective-permute-start(f32[64,128]{1,0:T(8,128)S(1)} %add.6), channel_id=1, source_target_pairs={{0,192},{192,0},{64,128},{128,64},{1,193},{193,1},{65,129},{129,65... | collective-permute-start | bytes 98312 | tf_op jit(solution)/shard_map/ppermute | solution.py:297
  32.4 0.5 %shard_map.122.refs_0_ = f32[768,128]{1,0:T(8,128)S(1)} custom-call(f32[544,256]{1,0:T(8,128)S(1)} %get-tuple-element.11.spec_ref, bf16[512,256]{1,0:T(8,128)(2,1)S(1)} %copy-done, f32[17,2,8,128]{3,2,1,0:T(8,128)S(1)} %copy-done.2, f32[17,2,8,128]{3,2,1,0:T(8,128)S(1)} %copy-done.1), custom_call_target="tpu_custom_call" | custom-call | tf_op jit(solution)/shard_map/pallas_call | solution.py:295
  32.9 0.8 %collective-permute-done.1 = f32[64,128]{1,0:T(8,128)S(1)} collective-permute-done((f32[64,128]{1,0:T(8,128)S(1)}, f32[64,128]{1,0:T(8,128)S(1)}, u32[]{:S(2)}, u32[]{:S(2)}) %collective-permute-start.1) | collective-permute-done | bytes 32800 | tf_op jit(solution)/shard_map/ppermute | solution.py:297
  33.7 0.0 copy-start.3
  33.7 0.0 copy-start.4
  33.7 0.0 copy-start.5
  33.8 17.8 %all_to_all.11 = f32[64,1,1536]{2,1,0:T(1,128)S(1)} all-to-all(f32[64,1,1536]{2,1,0:T(1,128)S(1)} %bitcast.12), channel_id=1, replica_groups=mesh['zh'=4,'y'=4,'x'=4,'zl'=2,'core'=2] {'y','x','zl','core'}, dimensions={0} | all-to-all | bytes 786432 | tf_op jit(solution)/shard_map/all_to_all | solution.py:281
  51.6 0.0 copy-done.3
  51.6 0.0 copy-done.4
  51.6 0.0 copy-done.5
  51.6 0.8 %shard_map.124 = (f32[128,256]{1,0:T(8,128)}, f32[128,256]{1,0:T(8,128)}, f32[128,256]{1,0:T(8,128)}, f32[128,256]{1,0:T(8,128)}) custom-call(f32[768,128]{1,0:T(8,128)S(1)} %bitcast.11, f32[128,256]{1,0:T(8,128)S(1)} %bitcast.16, f32[128,256]{1,0:T(8,128)S(1)} %bitcast.18, f32[128,256]{1,0:T(8,128)S(1)} %bitcast.20), custom_call_target="tpu_custom_call" | custom-call | tf_op jit(solution)/shard_map/pallas_call | solution.py:302
  (3 shorter events, 0.0 us)
Async XLA Ops:
  0.6 21.9 %copy-start.6 = (bf16[512,256]{1,0:T(8,128)(2,1)S(1)}, bf16[512,256]{1,0:T(8,128)(2,1)}, u32[]{:S(2)}) copy-start(bf16[512,256]{1,0:T(8,128)(2,1)} %constant.8.clone.forward_ref) | copy-start | bytes 786436
  1.9 20.7 %copy-start = (bf16[512,256]{1,0:T(8,128)(2,1)S(1)}, bf16[512,256]{1,0:T(8,128)(2,1)}, u32[]{:S(2)}) copy-start(bf16[512,256]{1,0:T(8,128)(2,1)} %constant.9.clone.inverse_ref) | copy-start | bytes 786436
  1.9 20.6 %copy-start.1 = (f32[17,2,8,128]{3,2,1,0:T(8,128)S(1)}, f32[17,2,8,128]{3,2,1,0:T(8,128)}, u32[]{:S(2)}) copy-start(f32[17,2,8,128]{3,2,1,0:T(8,128)} %constant.11.clone.rowfix_ref) | copy-start | bytes 417796
  1.9 20.6 %copy-start.2 = (f32[17,2,8,128]{3,2,1,0:T(8,128)S(1)}, f32[17,2,8,128]{3,2,1,0:T(8,128)}, u32[]{:S(2)}) copy-start(f32[17,2,8,128]{3,2,1,0:T(8,128)} %constant.10.clone.twiddle_ref) | copy-start | bytes 417796
  23.4 4.4 %collective-permute-start = (f32[64,128]{1,0:T(8,128)S(1)}, f32[64,128]{1,0:T(8,128)S(1)}, u32[]{:S(2)}, u32[]{:S(2)}) collective-permute-start(f32[64,128]{1,0:T(8,128)S(1)} %get-tuple-element.10), channel_id=1, source_target_pairs={{0,64},{64,0},{128,192},{192,128},{1,65},{65,1},{129,193},{193,129... | collective-permute-start | bytes 98312 | tf_op jit(solution)/shard_map/ppermute | solution.py:297
  27.8 5.9 %collective-permute-start.1 = (f32[64,128]{1,0:T(8,128)S(1)}, f32[64,128]{1,0:T(8,128)S(1)}, u32[]{:S(2)}, u32[]{:S(2)}) collective-permute-start(f32[64,128]{1,0:T(8,128)S(1)} %add.6), channel_id=1, source_target_pairs={{0,192},{192,0},{64,128},{128,64},{1,193},{193,1},{65,129},{129,65... | collective-permute-start | bytes 98312 | tf_op jit(solution)/shard_map/ppermute | solution.py:297
  33.7 17.9 %copy-start.3 = (f32[1,128,256]{2,1,0:T(8,128)S(1)}, f32[1,128,256]{2,1,0:T(8,128)}, u32[]{:S(2)}) copy-start(f32[1,128,256]{2,1,0:T(8,128)} %param.9) | copy-start | bytes 393220
  33.7 17.9 %copy-start.4 = (f32[1,128,256]{2,1,0:T(8,128)S(1)}, f32[1,128,256]{2,1,0:T(8,128)}, u32[]{:S(2)}) copy-start(f32[1,128,256]{2,1,0:T(8,128)} %param.10) | copy-start | bytes 393220
  33.7 17.8 %copy-start.5 = (f32[1,128,256]{2,1,0:T(8,128)S(1)}, f32[1,128,256]{2,1,0:T(8,128)}, u32[]{:S(2)}) copy-start(f32[1,128,256]{2,1,0:T(8,128)} %param.12) | copy-start | bytes 393220

commit v3 on v2

--- a/solution.py
+++ b/solution.py
@@ -9,7 +9,10 @@
 from jax.sharding import Mesh, PartitionSpec as P
 
 AXES = ("zh", "y", "x", "zl", "core")
-STEPS = [[(0, 1), (1, 0), (2, 3), (3, 2)], [(0, 3), (3, 0), (1, 2), (2, 1)]]
+STEPS = [
+    [(2 * zh + core, 2 * other + 1 - core) for zh, other in enumerate(order) for core in range(2)]
+    for order in ((3, 2, 1, 0), (1, 0, 3, 2))
+]
 FAR = ("y", "x", "zl", "core")
 BLOCKS = 17
 CLASSES = [0, 16, 8, 4, 20] + [8 * j + 2 for j in range(4)] + [4 * j + 1 for j in range(8)]
@@ -135,6 +138,11 @@
         target[start : start + step, :] = total
 
 
+def channel_bases():
+    odd = lax.axis_index("zh") % 2
+    return odd * 64, (1 - odd) * 64
+
+
 def pack_kernel(value_hbm, key_hbm, query_hbm, cot_hbm, filter_hbm, out_ref, value_ref, key_ref, query_ref, cot_ref, filter_ref, sems):
     copies = [
         pltpu.make_async_copy(value_hbm, value_ref, sems.at[0]),
@@ -145,21 +153,27 @@
     ]
     for copy in copies:
         copy.start()
-    y = lax.axis_index("y")
+    y, bases = lax.axis_index("y"), channel_bases()
     tap_half, tap_channel = y // 2, y % 2
     tap_lanes = pl.ds(pl.multiple_of(tap_half * 128, 128), 128)
-    tap_rows = pl.ds(pl.multiple_of(tap_channel * 64, 64), 64)
-    places = [(half * 4 + j, pl.ds(j * 64, 64), pl.ds(half * 128, 128)) for j in range(2) for half in range(2)]
+    places = [
+        (core * 9 + half * 4 + j, pl.ds(pl.multiple_of(bases[core] + j * 32, 32), 32), pl.ds(half * 128, 128))
+        for core in range(2)
+        for j in range(2)
+        for half in range(2)
+    ]
     copies[0].wait()
     copies[1].wait()
     for at, rows, lanes in places:
-        out_ref[pl.ds(at, 64, stride=9), :] = key_ref[rows, lanes] * value_ref[rows, lanes]
+        out_ref[pl.ds(at, 32, stride=18), :] = key_ref[rows, lanes] * value_ref[rows, lanes]
     copies[2].wait()
     copies[3].wait()
     for at, rows, lanes in places:
-        out_ref[pl.ds(at + 2, 64, stride=9), :] = cot_ref[rows, lanes] * query_ref[rows, lanes]
+        out_ref[pl.ds(at + 2, 32, stride=18), :] = cot_ref[rows, lanes] * query_ref[rows, lanes]
     copies[4].wait()
-    out_ref[pl.ds(8, 64, stride=9), :] = filter_ref[tap_rows, tap_lanes] * (1.0 / 64)
+    for core in range(2):
+        rows = pl.ds(pl.multiple_of(bases[core] + tap_channel * 32, 32), 32)
+        out_ref[pl.ds(core * 9 + 8, 32, stride=18), :] = filter_ref[rows, tap_lanes] * (1.0 / 64)
 
 
 def spectrum_rows(blocks, scratch, base, stride, sign, twiddle_ref, rowfix_ref):
@@ -251,17 +265,19 @@
 
 
 def unpack_kernel(signal_ref, value_ref, key_ref, cot_ref, query_out, key_out, value_out, filter_out):
-    for j in range(2):
-        rows = pl.ds(j * 64, 64)
-        for half in range(2):
-            lanes = pl.ds(half * 128, 128)
-            at = half * 4 + j
-            conv = signal_ref[pl.ds(at, 64, stride=12), :]
-            grad = signal_ref[pl.ds(at + 2, 64, stride=12), :]
-            query_out[rows, lanes] = cot_ref[rows, lanes] * conv
-            key_out[rows, lanes] = grad * value_ref[rows, lanes]
-            value_out[rows, lanes] = grad * key_ref[rows, lanes]
-            filter_out[rows, lanes] = signal_ref[pl.ds(8 + half * 2 + j, 64, stride=12), :]
+    bases = channel_bases()
+    for core in range(2):
+        for j in range(2):
+            rows = pl.ds(pl.multiple_of(bases[core] + j * 32, 32), 32)
+            for half in range(2):
+                lanes = pl.ds(half * 128, 128)
+                at = core * 12 + half * 4 + j
+                conv = signal_ref[pl.ds(at, 32, stride=24), :]
+                grad = signal_ref[pl.ds(at + 2, 32, stride=24), :]
+                query_out[rows, lanes] = cot_ref[rows, lanes] * conv
+                key_out[rows, lanes] = grad * value_ref[rows, lanes]
+                value_out[rows, lanes] = grad * key_ref[rows, lanes]
+                filter_out[rows, lanes] = signal_ref[pl.ds(core * 12 + 8 + half * 2 + j, 32, stride=24), :]
 
 
 def call(kernel, shapes, inputs, scratch=(), copies=0, **extra):
@@ -294,7 +310,7 @@
     )
     (message,) = call(inverse_kernel, [(768, 128)], 4, [(544, 256)])(spec, inverse, twiddle, rowfix)
     for pairs in STEPS:
-        part = part + lax.ppermute(part, "zh", pairs)
+        part = part + lax.ppermute(part, ("zh", "core"), pairs)
     parts = [part]
     (message,) = call(filter_kernel, [(768, 128)], 2)(*parts, message)
     signal = exchange(message.reshape(64, 1, 1536), FAR).reshape(768, 128)

time: 52.6 us -> 52 us (0.989)
  blocking collectives: 38.4 us -> 36.4 us
  waiting for transfers between devices: 2.07 us -> 3.08 us
    all_to_all x2, blocking collectives: 38.4 us -> 36.4 us  [exchange(): return lax.all_to_all(array, axes, split_axis=0, concat_axis=0, tiled=True)]
    ppermute x2, waiting for transfers between devices: 2.07 us -> 3.08 us  [on_device(): part = part + lax.ppermute(part, ('zh', 'core'), pairs)]
where the time goes in v3:
time: 52 us; the launch traced here: 51.8 us
  blocking collectives  36.4 us (70%)
  starting transfers between devices  8.01 us (15%)
  Pallas kernels  3.52 us (7%)
  waiting for transfers between devices  3.08 us (6%)
  between operations  0.73 us (1%)
    all_to_all x2, blocking collectives, exchange(): return lax.all_to_all(array, axes, split_axis=0, concat_axis=0, tiled=True)  36.4 us
    ppermute x2, starting transfers between devices, on_device(): part = part + lax.ppermute(part, ('zh', 'core'), pairs)  8.01 us
    ppermute x2, waiting for transfers between devices, on_device(): part = part + lax.ppermute(part, ('zh', 'core'), pairs)  3.08 us
    pallas_call x1, Pallas kernels, on_device(): call(pack_kernel, [(576, 128)], 5, [(128, 256)] * 5, copies=5)(*pinned)  1.25 us
  transfers between devices with their start and end apart: 2, of which 2 were waited for; matrix products, arithmetic and copies ran while one was open for 0% of the time, Pallas kernels for 1%

profile of v3, /device:TPU:1, one launch (start us, length us, event | category | flops | bytes accessed | tf_op | source)
XLA Modules:
  0.0 51.8 jit_solution(13051214489034819283)
XLA Ops:
  0.6 0.0 copy-start.6
  0.6 1.2 %shard_map.120 = f32[576,128]{1,0:T(8,128)S(1)} custom-call(f32[128,256]{1,0:T(8,128)} %bitcast.15, f32[128,256]{1,0:T(8,128)} %bitcast.17, f32[128,256]{1,0:T(8,128)} %bitcast.21, f32[128,256]{1,0:T(8,128)} %bitcast.19, f32[128,256]{1,0:T(8,128)} %filter_hbm.1), custom_call_target="tpu_custom_call" | custom-call | tf_op jit(solution)/shard_map/pallas_call | solution.py:304
  1.9 0.0 copy-start
  1.9 0.0 copy-start.1
  1.9 0.0 copy-start.2
  1.9 20.6 %all_to_all.10 = f32[64,1,1152]{2,1,0:T(1,128)S(1)} all-to-all(f32[64,1,1152]{2,1,0:T(1,128)S(1)} %bitcast.14), channel_id=1, replica_groups=mesh['zh'=4,'y'=4,'x'=4,'zl'=2,'core'=2] {'y','x','zl','core'}, dimensions={0} | all-to-all | bytes 589824 | tf_op jit(solution)/shard_map/all_to_all | solution.py:297
  22.6 0.0 copy-done.6
  22.6 0.0 copy-done
  22.6 0.0 copy-done.1
  22.6 0.0 copy-done.2
  22.6 0.8 %shard_map.121 = (f32[544,256]{1,0:T(8,128)S(1)}, f32[64,128]{1,0:T(8,128)S(1)}) custom-call(f32[576,128]{1,0:T(8,128)S(1)} %bitcast.13, bf16[512,256]{1,0:T(8,128)(2,1)S(1)} %copy-done.6, bf16[512,256]{1,0:T(8,128)(2,1)S(1)} %copy-done, f32[17,2,8,128]{3,2,1,0:T(8,128)S(1)} %copy-done.2, f32[17,2,8,128]{3,2,1,0:T(8,128)S(1)} %copy-done.1), custom_call_target="tpu_custom_call" | custom-call | tf_op jit(solution)/shard_map/pallas_call | solution.py:308
  23.4 5.6 %collective-permute-start = (f32[64,128]{1,0:T(8,128)S(1)}, f32[64,128]{1,0:T(8,128)S(1)}, u32[]{:S(2)}, u32[]{:S(2)}) collective-permute-start(f32[64,128]{1,0:T(8,128)S(1)} %get-tuple-element.10), channel_id=1, source_target_pairs={{0,193},{1,192},{64,129},{65,128},{128,65},{129,64},{192,1},{193,0... | collective-permute-start | bytes 98312 | tf_op jit(solution)/shard_map/ppermute | solution.py:313
  29.0 1.6 %collective-permute-done = f32[64,128]{1,0:T(8,128)S(1)} collective-permute-done((f32[64,128]{1,0:T(8,128)S(1)}, f32[64,128]{1,0:T(8,128)S(1)}, u32[]{:S(2)}, u32[]{:S(2)}) %collective-permute-start) | collective-permute-done | bytes 32800 | tf_op jit(solution)/shard_map/ppermute | solution.py:313
  30.6 2.5 %collective-permute-start.1 = (f32[64,128]{1,0:T(8,128)S(1)}, f32[64,128]{1,0:T(8,128)S(1)}, u32[]{:S(2)}, u32[]{:S(2)}) collective-permute-start(f32[64,128]{1,0:T(8,128)S(1)} %add.6), channel_id=1, source_target_pairs={{0,65},{1,64},{64,1},{65,0},{128,193},{129,192},{192,129},{193,128... | collective-permute-start | bytes 98312 | tf_op jit(solution)/shard_map/ppermute | solution.py:313
  33.0 0.5 %shard_map.122.refs_0_ = f32[768,128]{1,0:T(8,128)S(1)} custom-call(f32[544,256]{1,0:T(8,128)S(1)} %get-tuple-element.11.spec_ref, bf16[512,256]{1,0:T(8,128)(2,1)S(1)} %copy-done, f32[17,2,8,128]{3,2,1,0:T(8,128)S(1)} %copy-done.2, f32[17,2,8,128]{3,2,1,0:T(8,128)S(1)} %copy-done.1), custom_call_target="tpu_custom_call" | custom-call | tf_op jit(solution)/shard_map/pallas_call | solution.py:311
  33.6 1.5 %collective-permute-done.1 = f32[64,128]{1,0:T(8,128)S(1)} collective-permute-done((f32[64,128]{1,0:T(8,128)S(1)}, f32[64,128]{1,0:T(8,128)S(1)}, u32[]{:S(2)}, u32[]{:S(2)}) %collective-permute-start.1) | collective-permute-done | bytes 32800 | tf_op jit(solution)/shard_map/ppermute | solution.py:313
  35.1 0.0 copy-start.3
  35.1 0.0 copy-start.4
  35.1 0.0 copy-start.5
  35.1 15.8 %all_to_all.11 = f32[64,1,1536]{2,1,0:T(1,128)S(1)} all-to-all(f32[64,1,1536]{2,1,0:T(1,128)S(1)} %bitcast.12), channel_id=1, replica_groups=mesh['zh'=4,'y'=4,'x'=4,'zl'=2,'core'=2] {'y','x','zl','core'}, dimensions={0} | all-to-all | bytes 786432 | tf_op jit(solution)/shard_map/all_to_all | solution.py:297
  50.9 0.0 copy-done.3
  50.9 0.0 copy-done.4
  50.9 0.0 copy-done.5
  50.9 0.9 %shard_map.124 = (f32[128,256]{1,0:T(8,128)}, f32[128,256]{1,0:T(8,128)}, f32[128,256]{1,0:T(8,128)}, f32[128,256]{1,0:T(8,128)}) custom-call(f32[768,128]{1,0:T(8,128)S(1)} %bitcast.11, f32[128,256]{1,0:T(8,128)S(1)} %bitcast.16, f32[128,256]{1,0:T(8,128)S(1)} %bitcast.18, f32[128,256]{1,0:T(8,128)S(1)} %bitcast.20), custom_call_target="tpu_custom_call" | custom-call | tf_op jit(solution)/shard_map/pallas_call | solution.py:318
  (3 shorter events, 0.0 us)
Async XLA Ops:
  0.6 21.9 %copy-start.6 = (bf16[512,256]{1,0:T(8,128)(2,1)S(1)}, bf16[512,256]{1,0:T(8,128)(2,1)}, u32[]{:S(2)}) copy-start(bf16[512,256]{1,0:T(8,128)(2,1)} %constant.8.clone.forward_ref) | copy-start | bytes 786436
  1.9 20.7 %copy-start = (bf16[512,256]{1,0:T(8,128)(2,1)S(1)}, bf16[512,256]{1,0:T(8,128)(2,1)}, u32[]{:S(2)}) copy-start(bf16[512,256]{1,0:T(8,128)(2,1)} %constant.9.clone.inverse_ref) | copy-start | bytes 786436
  1.9 20.6 %copy-start.1 = (f32[17,2,8,128]{3,2,1,0:T(8,128)S(1)}, f32[17,2,8,128]{3,2,1,0:T(8,128)}, u32[]{:S(2)}) copy-start(f32[17,2,8,128]{3,2,1,0:T(8,128)} %constant.11.clone.rowfix_ref) | copy-start | bytes 417796
  1.9 20.6 %copy-start.2 = (f32[17,2,8,128]{3,2,1,0:T(8,128)S(1)}, f32[17,2,8,128]{3,2,1,0:T(8,128)}, u32[]{:S(2)}) copy-start(f32[17,2,8,128]{3,2,1,0:T(8,128)} %constant.10.clone.twiddle_ref) | copy-start | bytes 417796
  23.4 7.2 %collective-permute-start = (f32[64,128]{1,0:T(8,128)S(1)}, f32[64,128]{1,0:T(8,128)S(1)}, u32[]{:S(2)}, u32[]{:S(2)}) collective-permute-start(f32[64,128]{1,0:T(8,128)S(1)} %get-tuple-element.10), channel_id=1, source_target_pairs={{0,193},{1,192},{64,129},{65,128},{128,65},{129,64},{192,1},{193,0... | collective-permute-start | bytes 98312 | tf_op jit(solution)/shard_map/ppermute | solution.py:313
  30.6 4.5 %collective-permute-start.1 = (f32[64,128]{1,0:T(8,128)S(1)}, f32[64,128]{1,0:T(8,128)S(1)}, u32[]{:S(2)}, u32[]{:S(2)}) collective-permute-start(f32[64,128]{1,0:T(8,128)S(1)} %add.6), channel_id=1, source_target_pairs={{0,65},{1,64},{64,1},{65,0},{128,193},{129,192},{192,129},{193,128... | collective-permute-start | bytes 98312 | tf_op jit(solution)/shard_map/ppermute | solution.py:313
  35.1 15.8 %copy-start.3 = (f32[1,128,256]{2,1,0:T(8,128)S(1)}, f32[1,128,256]{2,1,0:T(8,128)}, u32[]{:S(2)}) copy-start(f32[1,128,256]{2,1,0:T(8,128)} %param.9) | copy-start | bytes 393220
  35.1 15.8 %copy-start.4 = (f32[1,128,256]{2,1,0:T(8,128)S(1)}, f32[1,128,256]{2,1,0:T(8,128)}, u32[]{:S(2)}) copy-start(f32[1,128,256]{2,1,0:T(8,128)} %param.10) | copy-start | bytes 393220
  35.1 15.8 %copy-start.5 = (f32[1,128,256]{2,1,0:T(8,128)S(1)}, f32[1,128,256]{2,1,0:T(8,128)}, u32[]{:S(2)}) copy-start(f32[1,128,256]{2,1,0:T(8,128)} %param.12) | copy-start | bytes 393220

commit v4 on v3

--- a/solution.py
+++ b/solution.py
@@ -9,9 +9,14 @@
 from jax.sharding import Mesh, PartitionSpec as P
 
 AXES = ("zh", "y", "x", "zl", "core")
+ORDERS = ((3, 2, 1, 0), (1, 0, 3, 2))
 STEPS = [
-    [(2 * zh + core, 2 * other + 1 - core) for zh, other in enumerate(order) for core in range(2)]
-    for order in ((3, 2, 1, 0), (1, 0, 3, 2))
+    [
+        (2 * zh + core, 2 * ORDERS[(step + core + zh + 0) % 2][zh] + 1 - core)
+        for zh in range(4)
+        for core in range(2)
+    ]
+    for step in range(2)
 ]
 FAR = ("y", "x", "zl", "core")
 BLOCKS = 17
@@ -126,16 +131,15 @@
     return (a[0] * sign + swap_halves(a[0]), a[1] * sign + swap_halves(a[1]))
 
 
-def multiply(source, target, table, rows, step):
+def multiply(source, target, table, start):
     high_table, low_table = table[0:256, :], table[256:512, :]
-    for start in range(0, rows, step):
-        block = source[start : start + step, :]
-        high = block.astype(jnp.bfloat16)
-        low = (block - high.astype(jnp.float32)).astype(jnp.bfloat16)
-        total = jnp.dot(high, low_table, preferred_element_type=jnp.float32)
-        total += jnp.dot(low, high_table, preferred_element_type=jnp.float32)
-        total += jnp.dot(high, high_table, preferred_element_type=jnp.float32)
-        target[start : start + step, :] = total
+    block = source[start : start + 136, :]
+    high = block.astype(jnp.bfloat16)
+    low = (block - high.astype(jnp.float32)).astype(jnp.bfloat16)
+    total = jnp.dot(high, low_table, preferred_element_type=jnp.float32)
+    total += jnp.dot(low, high_table, preferred_element_type=jnp.float32)
+    total += jnp.dot(high, high_table, preferred_element_type=jnp.float32)
+    target[start : start + 136, :] = total
 
 
 def channel_bases():
@@ -176,7 +180,7 @@
         out_ref[pl.ds(core * 9 + 8, 32, stride=18), :] = filter_ref[rows, tap_lanes] * (1.0 / 64)
 
 
-def spectrum_rows(blocks, scratch, base, stride, sign, twiddle_ref, rowfix_ref):
+def spectrum_rows(blocks, scratch, base, sign, twiddle_ref, rowfix_ref):
     for index, value in enumerate(blocks_forward(blocks)):
         fix = (rowfix_ref[index, 0], rowfix_ref[index, 1])
         if value[1] is None:
@@ -185,15 +189,15 @@
             value = times(value, fix)
         value = butterfly(value, sign)
         value = times(value, (twiddle_ref[index, 0], twiddle_ref[index, 1]))
-        at = base + index * stride
+        at = base + index * 8
         scratch[at : at + 8, 0:128] = value[0]
         scratch[at : at + 8, 128:256] = value[1]
 
 
-def blocks_of(scratch, base, stride, sign, twiddle_ref, rowfix_ref):
+def blocks_of(scratch, base, sign, twiddle_ref, rowfix_ref):
     spectrum = []
     for index in range(BLOCKS):
-        at = base + index * stride
+        at = base + index * 8
         value = (scratch[at : at + 8, 0:128], scratch[at : at + 8, 128:256])
         value = times(value, (twiddle_ref[index, 0], twiddle_ref[index, 1]), True)
         value = butterfly(value, sign)
@@ -201,7 +205,31 @@
     return blocks_inverse(spectrum)
 
 
-def forward_kernel(signal_ref, forward_ref, inverse_ref, twiddle_ref, rowfix_ref, spec_ref, part_ref, raw, spec, taps):
+def forward_kernel(signal_ref, forward_ref, inverse_ref, twiddle_ref, rowfix_ref, spec_ref, part_ref, raw):
+    sign = half_sign()
+    for y in range(4):
+        blocks = [signal_ref[(y * 16 + c) * 9 : (y * 16 + c) * 9 + 8, :] for c in range(16)]
+        spectrum_rows(blocks, raw, y * 136, sign, twiddle_ref, rowfix_ref)
+        multiply(raw, spec_ref, forward_ref, y * 136)
+    for index in range(BLOCKS):
+        total = None
+        for y in range(4):
+            at = y * 136 + index * 8
+            value = (spec_ref[at : at + 8, 0:128], spec_ref[at : at + 8, 128:256])
+            weight = (pltpu.roll(value[0], 6, 0), pltpu.roll(value[1], 6, 0))
+            term = times(weight, value, True)
+            total = term if total is None else add(total, term)
+        raw[544 + index * 8 : 552 + index * 8, 0:128] = total[0]
+        raw[544 + index * 8 : 552 + index * 8, 128:256] = total[1]
+    multiply(raw, raw, inverse_ref, 544)
+    blocks = blocks_of(raw, 544, sign, twiddle_ref, rowfix_ref)
+    for c in range(16):
+        for half in range(2):
+            at = c * 4 + half * 2
+            part_ref[at : at + 2, :] = blocks[c][half * 4 : half * 4 + 2, :]
+
+
+def inverse_kernel(signal_ref, spec_ref, forward_ref, inverse_ref, twiddle_ref, rowfix_ref, out_ref, raw, spec, taps):
     sign = half_sign()
     for y in range(4):
         at = (y // 2) * 4 + y % 2
@@ -209,42 +237,20 @@
             rows = signal_ref[pl.ds((y * 16 + c) * 9 + 8, 8, stride=9), :]
             taps[pl.ds(c * 8 + at, 8, stride=8), :] = rows
             taps[pl.ds(c * 8 + at + 2, 8, stride=8), :] = rows
-    spectrum_rows([taps[c * 8 : c * 8 + 8, :] for c in range(16)], raw, 544, 8, sign, twiddle_ref, rowfix_ref)
-    for y in range(4):
-        blocks = [signal_ref[(y * 16 + c) * 9 : (y * 16 + c) * 9 + 8, :] for c in range(16)]
-        spectrum_rows(blocks, raw, y * 8, 32, sign, twiddle_ref, rowfix_ref)
-    multiply(raw, spec, forward_ref, 680, 136)
+    spectrum_rows([taps[c * 8 : c * 8 + 8, :] for c in range(16)], raw, 544, sign, twiddle_ref, rowfix_ref)
+    multiply(raw, spec, forward_ref, 544)
     rows = lax.broadcasted_iota(jnp.int32, (8, 128), 0)
     flip = jnp.where(rows % 4 < 2, 1.0, -1.0).astype(jnp.float32)
-    for index in range(BLOCKS):
-        at = 544 + index * 8
-        tap = (spec[at : at + 8, 0:128], spec[at : at + 8, 128:256] * flip)
-        total = None
-        for y in range(4):
-            at = index * 32 + y * 8
-            value = (spec[at : at + 8, 0:128], spec[at : at + 8, 128:256])
-            product = times(value, tap)
-            spec_ref[at : at + 8, 0:128] = product[0]
-            spec_ref[at : at + 8, 128:256] = product[1]
-            weight = (pltpu.roll(value[0], 6, 0), pltpu.roll(value[1], 6, 0))
-            term = times(weight, value, True)
-            total = term if total is None else add(total, term)
-        raw[index * 8 : index * 8 + 8, 0:128] = total[0]
-        raw[index * 8 : index * 8 + 8, 128:256] = total[1]
-    multiply(raw, spec, inverse_ref, 136, 136)
-    blocks = blocks_of(spec, 0, 8, sign, twiddle_ref, rowfix_ref)
-    for c in range(16):
-        for half in range(2):
-            rows2 = blocks[c][half * 4 : half * 4 + 2, :]
-            at = c * 4 + half * 2
-            part_ref[at : at + 2, :] = rows2
-
-
-def inverse_kernel(spec_ref, inverse_ref, twiddle_ref, rowfix_ref, out_ref, raw):
-    sign = half_sign()
-    multiply(spec_ref, raw, inverse_ref, 544, 136)
     for y in range(4):
-        blocks = blocks_of(raw, y * 8, 32, sign, twiddle_ref, rowfix_ref)
+        for index in range(BLOCKS):
+            at = 544 + index * 8
+            tap = (spec[at : at + 8, 0:128], spec[at : at + 8, 128:256] * flip)
+            at = y * 136 + index * 8
+            value = times((spec_ref[at : at + 8, 0:128], spec_ref[at : at + 8, 128:256]), tap)
+            raw[at : at + 8, 0:128] = value[0]
+            raw[at : at + 8, 128:256] = value[1]
+        multiply(raw, spec, inverse_ref, y * 136)
+        blocks = blocks_of(spec, y * 136, sign, twiddle_ref, rowfix_ref)
         for c in range(16):
             at = (y * 16 + c) * 12
             out_ref[at : at + 8, :] = blocks[c]
@@ -305,14 +311,15 @@
         *pinned
     )
     signal = exchange(message.reshape(64, 1, 1152), FAR).reshape(576, 128)
-    spec, part = call(forward_kernel, [(544, 256), (64, 128)], 5, [(680, 256), (680, 256), (128, 128)])(
+    spec, part = call(forward_kernel, [(544, 256), (64, 128)], 5, [(680, 256)])(
         signal, forward, inverse, twiddle, rowfix
     )
-    (message,) = call(inverse_kernel, [(768, 128)], 4, [(544, 256)])(spec, inverse, twiddle, rowfix)
     for pairs in STEPS:
         part = part + lax.ppermute(part, ("zh", "core"), pairs)
-    parts = [part]
-    (message,) = call(filter_kernel, [(768, 128)], 2)(*parts, message)
+    (message,) = call(inverse_kernel, [(768, 128)], 6, [(680, 256)] * 2 + [(128, 128)])(
+        signal, spec, forward, inverse, twiddle, rowfix
+    )
+    (message,) = call(filter_kernel, [(768, 128)], 2)(part, message)
     signal = exchange(message.reshape(64, 1, 1536), FAR).reshape(768, 128)
     shape = (128, 256)
     query_grad, key_grad, value_grad, filter_grad = call(unpack_kernel, [shape] * 4, 4)(

time: 52 us -> 51.3 us (0.987)
  waiting for transfers between devices: 3.08 us -> 2.52 us
    ppermute x2, waiting for transfers between devices: 3.08 us -> 2.52 us  [on_device(): part = part + lax.ppermute(part, ('zh', 'core'), pairs)]
where the time goes in v4:
time: 51.3 us; the launch traced here: 51.1 us
  blocking collectives  35.9 us (70%)
  starting transfers between devices  8.13 us (16%)
  Pallas kernels  3.69 us (7%)
  waiting for transfers between devices  2.52 us (5%)
  between operations  0.73 us (1%)
    all_to_all x2, blocking collectives, exchange(): return lax.all_to_all(array, axes, split_axis=0, concat_axis=0, tiled=True)  35.9 us
    ppermute x2, starting transfers between devices, on_device(): part = part + lax.ppermute(part, ('zh', 'core'), pairs)  8.13 us
    ppermute x2, waiting for transfers between devices, on_device(): part = part + lax.ppermute(part, ('zh', 'core'), pairs)  2.52 us
    pallas_call x1, Pallas kernels, on_device(): call(pack_kernel, [(576, 128)], 5, [(128, 256)] * 5, copies=5)(*pinned)  1.25 us
  transfers between devices with their start and end apart: 2, of which 2 were waited for; matrix products, arithmetic and copies ran while one was open for 0% of the time, Pallas kernels for 1%

profile of v4, /device:TPU:1, one launch (start us, length us, event | category | flops | bytes accessed | tf_op | source)
XLA Modules:
  0.0 51.1 jit_solution(13581013844992489216)
XLA Ops:
  0.6 0.0 copy-start.2
  0.6 0.0 copy-start.3
  0.7 1.2 %shard_map.120 = f32[576,128]{1,0:T(8,128)S(1)} custom-call(f32[128,256]{1,0:T(8,128)} %bitcast.16, f32[128,256]{1,0:T(8,128)} %bitcast.18, f32[128,256]{1,0:T(8,128)} %bitcast.22, f32[128,256]{1,0:T(8,128)} %bitcast.20, f32[128,256]{1,0:T(8,128)} %filter_hbm.1), custom_call_target="tpu_custom_call" | custom-call | tf_op jit(solution)/shard_map/pallas_call | solution.py:310
  1.9 0.0 copy-start
  1.9 0.0 copy-start.1
  1.9 20.6 %all_to_all.10 = f32[64,1,1152]{2,1,0:T(1,128)S(1)} all-to-all(f32[64,1,1152]{2,1,0:T(1,128)S(1)} %bitcast.15), channel_id=1, replica_groups=mesh['zh'=4,'y'=4,'x'=4,'zl'=2,'core'=2] {'y','x','zl','core'}, dimensions={0} | all-to-all | bytes 589824 | tf_op jit(solution)/shard_map/all_to_all | solution.py:303
  22.6 0.0 copy-done.2
  22.6 0.0 copy-done.3
  22.6 0.0 copy-done
  22.6 0.0 copy-done.1
  22.6 0.8 %shard_map.121 = (f32[544,256]{1,0:T(8,128)S(1)}, f32[64,128]{1,0:T(8,128)S(1)}) custom-call(f32[576,128]{1,0:T(8,128)S(1)} %bitcast.11, bf16[512,256]{1,0:T(8,128)(2,1)S(1)} %copy-done.1, bf16[512,256]{1,0:T(8,128)(2,1)S(1)} %copy-done, f32[17,2,8,128]{3,2,1,0:T(8,128)S(1)} %copy-done.3, f32[17,2,8,128]{3,2,1,0:T(8,128)S(1)} %copy-done.2), custom_call_target="tpu_custom_call" | custom-call | tf_op jit(solution)/shard_map/pallas_call | solution.py:314
  23.4 3.4 %collective-permute-start = (f32[64,128]{1,0:T(8,128)S(1)}, f32[64,128]{1,0:T(8,128)S(1)}, u32[]{:S(2)}, u32[]{:S(2)}) collective-permute-start(f32[64,128]{1,0:T(8,128)S(1)} %get-tuple-element.10), channel_id=1, source_target_pairs={{0,193},{1,64},{64,1},{65,128},{128,65},{129,192},{192,129},{193,0... | collective-permute-start | bytes 98312 | tf_op jit(solution)/shard_map/ppermute | solution.py:318
  26.8 1.7 %collective-permute-done = f32[64,128]{1,0:T(8,128)S(1)} collective-permute-done((f32[64,128]{1,0:T(8,128)S(1)}, f32[64,128]{1,0:T(8,128)S(1)}, u32[]{:S(2)}, u32[]{:S(2)}) %collective-permute-start) | collective-permute-done | bytes 32800 | tf_op jit(solution)/shard_map/ppermute | solution.py:318
  28.5 4.7 %collective-permute-start.1 = (f32[64,128]{1,0:T(8,128)S(1)}, f32[64,128]{1,0:T(8,128)S(1)}, u32[]{:S(2)}, u32[]{:S(2)}) collective-permute-start(f32[64,128]{1,0:T(8,128)S(1)} %add.6), channel_id=1, source_target_pairs={{0,65},{1,192},{64,129},{65,0},{128,193},{129,64},{192,1},{193,128... | collective-permute-start | bytes 98312 | tf_op jit(solution)/shard_map/ppermute | solution.py:318
  33.2 0.7 %shard_map.122.refs_0_ = f32[768,128]{1,0:T(8,128)S(1)} custom-call(f32[576,128]{1,0:T(8,128)S(1)} %bitcast.12, f32[544,256]{1,0:T(8,128)S(1)} %get-tuple-element.11.spec_ref, bf16[512,256]{1,0:T(8,128)(2,1)S(1)} %copy-done.1, bf16[512,256]{1,0:T(8,128)(2,1)S(1)} %copy-done, f32[17,2,8,128]{3,2,1,0:T(8,128)S(1)} %copy-done.3, f32[17,2,8,128]{3,2,1,0:T(8,128)S(1)} %copy-done.2), custom_call_target="tpu_custom_call" | custom-call | tf_op jit(solution)/shard_map/pallas_call | solution.py:319
  33.9 0.9 %collective-permute-done.1 = f32[64,128]{1,0:T(8,128)S(1)} collective-permute-done((f32[64,128]{1,0:T(8,128)S(1)}, f32[64,128]{1,0:T(8,128)S(1)}, u32[]{:S(2)}, u32[]{:S(2)}) %collective-permute-start.1) | collective-permute-done | bytes 32800 | tf_op jit(solution)/shard_map/ppermute | solution.py:318
  34.8 0.0 copy-start.4
  34.8 0.0 copy-start.5
  34.8 0.0 copy-start.6
  34.9 15.3 %all_to_all.11 = f32[64,1,1536]{2,1,0:T(1,128)S(1)} all-to-all(f32[64,1,1536]{2,1,0:T(1,128)S(1)} %bitcast.14), channel_id=1, replica_groups=mesh['zh'=4,'y'=4,'x'=4,'zl'=2,'core'=2] {'y','x','zl','core'}, dimensions={0} | all-to-all | bytes 786432 | tf_op jit(solution)/shard_map/all_to_all | solution.py:303
  50.2 0.0 copy-done.4
  50.2 0.0 copy-done.5
  50.2 0.0 copy-done.6
  50.2 0.9 %shard_map.124 = (f32[128,256]{1,0:T(8,128)}, f32[128,256]{1,0:T(8,128)}, f32[128,256]{1,0:T(8,128)}, f32[128,256]{1,0:T(8,128)}) custom-call(f32[768,128]{1,0:T(8,128)S(1)} %bitcast.13, f32[128,256]{1,0:T(8,128)S(1)} %bitcast.17, f32[128,256]{1,0:T(8,128)S(1)} %bitcast.19, f32[128,256]{1,0:T(8,128)S(1)} %bitcast.21), custom_call_target="tpu_custom_call" | custom-call | tf_op jit(solution)/shard_map/pallas_call | solution.py:325
  (3 shorter events, 0.0 us)
Async XLA Ops:
  0.6 21.9 %copy-start.2 = (f32[17,2,8,128]{3,2,1,0:T(8,128)S(1)}, f32[17,2,8,128]{3,2,1,0:T(8,128)}, u32[]{:S(2)}) copy-start(f32[17,2,8,128]{3,2,1,0:T(8,128)} %constant.11.clone.rowfix_ref) | copy-start | bytes 417796
  0.6 21.9 %copy-start.3 = (f32[17,2,8,128]{3,2,1,0:T(8,128)S(1)}, f32[17,2,8,128]{3,2,1,0:T(8,128)}, u32[]{:S(2)}) copy-start(f32[17,2,8,128]{3,2,1,0:T(8,128)} %constant.10.clone.twiddle_ref) | copy-start | bytes 417796
  1.9 20.6 %copy-start = (bf16[512,256]{1,0:T(8,128)(2,1)S(1)}, bf16[512,256]{1,0:T(8,128)(2,1)}, u32[]{:S(2)}) copy-start(bf16[512,256]{1,0:T(8,128)(2,1)} %constant.9.clone.inverse_ref) | copy-start | bytes 786436
  1.9 20.6 %copy-start.1 = (bf16[512,256]{1,0:T(8,128)(2,1)S(1)}, bf16[512,256]{1,0:T(8,128)(2,1)}, u32[]{:S(2)}) copy-start(bf16[512,256]{1,0:T(8,128)(2,1)} %constant.8.clone.forward_ref) | copy-start | bytes 786436
  23.4 5.1 %collective-permute-start = (f32[64,128]{1,0:T(8,128)S(1)}, f32[64,128]{1,0:T(8,128)S(1)}, u32[]{:S(2)}, u32[]{:S(2)}) collective-permute-start(f32[64,128]{1,0:T(8,128)S(1)} %get-tuple-element.10), channel_id=1, source_target_pairs={{0,193},{1,64},{64,1},{65,128},{128,65},{129,192},{192,129},{193,0... | collective-permute-start | bytes 98312 | tf_op jit(solution)/shard_map/ppermute | solution.py:318
  28.5 6.3 %collective-permute-start.1 = (f32[64,128]{1,0:T(8,128)S(1)}, f32[64,128]{1,0:T(8,128)S(1)}, u32[]{:S(2)}, u32[]{:S(2)}) collective-permute-start(f32[64,128]{1,0:T(8,128)S(1)} %add.6), channel_id=1, source_target_pairs={{0,65},{1,192},{64,129},{65,0},{128,193},{129,64},{192,1},{193,128... | collective-permute-start | bytes 98312 | tf_op jit(solution)/shard_map/ppermute | solution.py:318
  34.8 15.4 %copy-start.4 = (f32[1,128,256]{2,1,0:T(8,128)S(1)}, f32[1,128,256]{2,1,0:T(8,128)}, u32[]{:S(2)}) copy-start(f32[1,128,256]{2,1,0:T(8,128)} %param.9) | copy-start | bytes 393220
  34.8 15.4 %copy-start.5 = (f32[1,128,256]{2,1,0:T(8,128)S(1)}, f32[1,128,256]{2,1,0:T(8,128)}, u32[]{:S(2)}) copy-start(f32[1,128,256]{2,1,0:T(8,128)} %param.10) | copy-start | bytes 393220
  34.8 15.3 %copy-start.6 = (f32[1,128,256]{2,1,0:T(8,128)S(1)}, f32[1,128,256]{2,1,0:T(8,128)}, u32[]{:S(2)}) copy-start(f32[1,128,256]{2,1,0:T(8,128)} %param.12) | copy-start | bytes 393220

commit v5 on v4

--- a/solution.py
+++ b/solution.py
@@ -37,7 +37,7 @@
     def split(table):
         high = table.astype(np.float32).astype(jnp.bfloat16)
         low = (table - high.astype(np.float64)).astype(np.float32).astype(jnp.bfloat16)
-        return np.concatenate([high, low], 0)
+        return np.concatenate([high, high, low], 0)
 
     row_half = np.arange(8) // 4
     twiddle = np.zeros((BLOCKS, 2, 8, 128), np.float32)
@@ -132,14 +132,11 @@
 
 
 def multiply(source, target, table, start):
-    high_table, low_table = table[0:256, :], table[256:512, :]
     block = source[start : start + 136, :]
     high = block.astype(jnp.bfloat16)
     low = (block - high.astype(jnp.float32)).astype(jnp.bfloat16)
-    total = jnp.dot(high, low_table, preferred_element_type=jnp.float32)
-    total += jnp.dot(low, high_table, preferred_element_type=jnp.float32)
-    total += jnp.dot(high, high_table, preferred_element_type=jnp.float32)
-    target[start : start + 136, :] = total
+    parts = jnp.concatenate([high, low, high], 1)
+    target[start : start + 136, :] = jnp.dot(parts, table[...], preferred_element_type=jnp.float32)
 
 
 def channel_bases():
@@ -153,13 +150,15 @@
         pltpu.make_async_copy(key_hbm, key_ref, sems.at[1]),
         pltpu.make_async_copy(cot_hbm, cot_ref, sems.at[2]),
         pltpu.make_async_copy(query_hbm, query_ref, sems.at[3]),
-        pltpu.make_async_copy(filter_hbm, filter_ref, sems.at[4]),
     ]
     for copy in copies:
         copy.start()
     y, bases = lax.axis_index("y"), channel_bases()
-    tap_half, tap_channel = y // 2, y % 2
-    tap_lanes = pl.ds(pl.multiple_of(tap_half * 128, 128), 128)
+    lanes = pl.ds(pl.multiple_of((y // 2) * 128, 128), 128)
+    for core in range(2):
+        rows = pl.ds(pl.multiple_of(bases[core] + (y % 2) * 32, 32), 32)
+        copies.append(pltpu.make_async_copy(filter_hbm.at[rows, lanes], filter_ref.at[core], sems.at[4 + core]))
+        copies[-1].start()
     places = [
         (core * 9 + half * 4 + j, pl.ds(pl.multiple_of(bases[core] + j * 32, 32), 32), pl.ds(half * 128, 128))
         for core in range(2)
@@ -174,10 +173,9 @@
     copies[3].wait()
     for at, rows, lanes in places:
         out_ref[pl.ds(at + 2, 32, stride=18), :] = cot_ref[rows, lanes] * query_ref[rows, lanes]
-    copies[4].wait()
     for core in range(2):
-        rows = pl.ds(pl.multiple_of(bases[core] + tap_channel * 32, 32), 32)
-        out_ref[pl.ds(core * 9 + 8, 32, stride=18), :] = filter_ref[rows, tap_lanes] * (1.0 / 64)
+        copies[4 + core].wait()
+        out_ref[pl.ds(core * 9 + 8, 32, stride=18), :] = filter_ref[core] * (1.0 / 64)
 
 
 def spectrum_rows(blocks, scratch, base, sign, twiddle_ref, rowfix_ref):
@@ -307,7 +305,7 @@
     value_in, key_in, query_in, cotangent = value_in[0], key_in[0], query_in[0], cotangent[0]
     forward, inverse, twiddle, rowfix = [jnp.asarray(table) for table in tables()]
     pinned = [pltpu.with_memory_space_constraint(a, pltpu.HBM) for a in (value_in, key_in, query_in, cotangent, filter_param)]
-    (message,) = call(pack_kernel, [(576, 128)], 5, [(128, 256)] * 5, copies=5)(
+    (message,) = call(pack_kernel, [(576, 128)], 5, [(128, 256)] * 4 + [(2, 32, 128)], copies=6)(
         *pinned
     )
     signal = exchange(message.reshape(64, 1, 1152), FAR).reshape(576, 128)

time: 51.3 us -> 51.2 us (level)
  no operation moved by 1% of the time
where the time goes in v5:
time: 51.2 us; the launch traced here: 51 us
  blocking collectives  35.9 us (70%)
  starting transfers between devices  8.13 us (16%)
  Pallas kernels  3.67 us (7%)
  waiting for transfers between devices  2.51 us (5%)
  between operations  0.73 us (1%)
    all_to_all x2, blocking collectives, exchange(): return lax.all_to_all(array, axes, split_axis=0, concat_axis=0, tiled=True)  35.9 us
    ppermute x2, starting transfers between devices, on_device(): part = part + lax.ppermute(part, ('zh', 'core'), pairs)  8.13 us
    ppermute x2, waiting for transfers between devices, on_device(): part = part + lax.ppermute(part, ('zh', 'core'), pairs)  2.51 us
    pallas_call x1, Pallas kernels, on_device(): call(pack_kernel, [(576, 128)], 5, [(128, 256)] * 4 + [(2, 32, 128)], cop...  1.23 us
  transfers between devices with their start and end apart: 2, of which 2 were waited for; matrix products, arithmetic and copies ran while one was open for 0% of the time, Pallas kernels for 1%

profile of v5, /device:TPU:1, one launch (start us, length us, event | category | flops | bytes accessed | tf_op | source)
XLA Modules:
  0.0 51.0 jit_solution(6382921805913692647)
XLA Ops:
  0.6 0.0 copy-start.1
  0.6 0.0 copy-start.3
  0.7 1.2 %shard_map.120 = f32[576,128]{1,0:T(8,128)S(1)} custom-call(f32[128,256]{1,0:T(8,128)} %bitcast.16, f32[128,256]{1,0:T(8,128)} %bitcast.18, f32[128,256]{1,0:T(8,128)} %bitcast.22, f32[128,256]{1,0:T(8,128)} %bitcast.20, f32[128,256]{1,0:T(8,128)} %filter_hbm.1), custom_call_target="tpu_custom_call" | custom-call | tf_op jit(solution)/shard_map/pallas_call | solution.py:308
  1.9 0.0 copy-start
  1.9 0.0 copy-start.2
  1.9 20.6 %all_to_all.10 = f32[64,1,1152]{2,1,0:T(1,128)S(1)} all-to-all(f32[64,1,1152]{2,1,0:T(1,128)S(1)} %bitcast.15), channel_id=1, replica_groups=mesh['zh'=4,'y'=4,'x'=4,'zl'=2,'core'=2] {'y','x','zl','core'}, dimensions={0} | all-to-all | bytes 589824 | tf_op jit(solution)/shard_map/all_to_all | solution.py:301
  22.5 0.0 copy-done.1
  22.5 0.0 copy-done.3
  22.5 0.0 copy-done
  22.5 0.0 copy-done.2
  22.6 0.8 %shard_map.121 = (f32[544,256]{1,0:T(8,128)S(1)}, f32[64,128]{1,0:T(8,128)S(1)}) custom-call(f32[576,128]{1,0:T(8,128)S(1)} %bitcast.11, bf16[768,256]{1,0:T(8,128)(2,1)S(1)} %copy-done.1, bf16[768,256]{1,0:T(8,128)(2,1)S(1)} %copy-done, f32[17,2,8,128]{3,2,1,0:T(8,128)S(1)} %copy-done.3, f32[17,2,8,128]{3,2,1,0:T(8,128)S(1)} %copy-done.2), custom_call_target="tpu_custom_call" | custom-call | tf_op jit(solution)/shard_map/pallas_call | solution.py:312
  23.4 3.4 %collective-permute-start = (f32[64,128]{1,0:T(8,128)S(1)}, f32[64,128]{1,0:T(8,128)S(1)}, u32[]{:S(2)}, u32[]{:S(2)}) collective-permute-start(f32[64,128]{1,0:T(8,128)S(1)} %get-tuple-element.10), channel_id=1, source_target_pairs={{0,193},{1,64},{64,1},{65,128},{128,65},{129,192},{192,129},{193,0... | collective-permute-start | bytes 98312 | tf_op jit(solution)/shard_map/ppermute | solution.py:316
  26.8 1.7 %collective-permute-done = f32[64,128]{1,0:T(8,128)S(1)} collective-permute-done((f32[64,128]{1,0:T(8,128)S(1)}, f32[64,128]{1,0:T(8,128)S(1)}, u32[]{:S(2)}, u32[]{:S(2)}) %collective-permute-start) | collective-permute-done | bytes 32800 | tf_op jit(solution)/shard_map/ppermute | solution.py:316
  28.4 4.7 %collective-permute-start.1 = (f32[64,128]{1,0:T(8,128)S(1)}, f32[64,128]{1,0:T(8,128)S(1)}, u32[]{:S(2)}, u32[]{:S(2)}) collective-permute-start(f32[64,128]{1,0:T(8,128)S(1)} %add.6), channel_id=1, source_target_pairs={{0,65},{1,192},{64,129},{65,0},{128,193},{129,64},{192,1},{193,128... | collective-permute-start | bytes 98312 | tf_op jit(solution)/shard_map/ppermute | solution.py:316
  33.1 0.7 %shard_map.122.refs_0_ = f32[768,128]{1,0:T(8,128)S(1)} custom-call(f32[576,128]{1,0:T(8,128)S(1)} %bitcast.12, f32[544,256]{1,0:T(8,128)S(1)} %get-tuple-element.11.spec_ref, bf16[768,256]{1,0:T(8,128)(2,1)S(1)} %copy-done.1, bf16[768,256]{1,0:T(8,128)(2,1)S(1)} %copy-done, f32[17,2,8,128]{3,2,1,0:T(8,128)S(1)} %copy-done.3, f32[17,2,8,128]{3,2,1,0:T(8,128)S(1)} %copy-done.2), custom_call_target="tpu_custom_call" | custom-call | tf_op jit(solution)/shard_map/pallas_call | solution.py:317
  33.9 0.8 %collective-permute-done.1 = f32[64,128]{1,0:T(8,128)S(1)} collective-permute-done((f32[64,128]{1,0:T(8,128)S(1)}, f32[64,128]{1,0:T(8,128)S(1)}, u32[]{:S(2)}, u32[]{:S(2)}) %collective-permute-start.1) | collective-permute-done | bytes 32800 | tf_op jit(solution)/shard_map/ppermute | solution.py:316
  34.8 0.0 copy-start.4
  34.8 0.0 copy-start.5
  34.8 0.0 copy-start.6
  34.8 15.3 %all_to_all.11 = f32[64,1,1536]{2,1,0:T(1,128)S(1)} all-to-all(f32[64,1,1536]{2,1,0:T(1,128)S(1)} %bitcast.14), channel_id=1, replica_groups=mesh['zh'=4,'y'=4,'x'=4,'zl'=2,'core'=2] {'y','x','zl','core'}, dimensions={0} | all-to-all | bytes 786432 | tf_op jit(solution)/shard_map/all_to_all | solution.py:301
  50.1 0.0 copy-done.4
  50.2 0.0 copy-done.5
  50.2 0.0 copy-done.6
  50.2 0.9 %shard_map.124 = (f32[128,256]{1,0:T(8,128)}, f32[128,256]{1,0:T(8,128)}, f32[128,256]{1,0:T(8,128)}, f32[128,256]{1,0:T(8,128)}) custom-call(f32[768,128]{1,0:T(8,128)S(1)} %bitcast.13, f32[128,256]{1,0:T(8,128)S(1)} %bitcast.17, f32[128,256]{1,0:T(8,128)S(1)} %bitcast.19, f32[128,256]{1,0:T(8,128)S(1)} %bitcast.21), custom_call_target="tpu_custom_call" | custom-call | tf_op jit(solution)/shard_map/pallas_call | solution.py:323
  (3 shorter events, 0.0 us)
Async XLA Ops:
  0.6 21.9 %copy-start.1 = (bf16[768,256]{1,0:T(8,128)(2,1)S(1)}, bf16[768,256]{1,0:T(8,128)(2,1)}, u32[]{:S(2)}) copy-start(bf16[768,256]{1,0:T(8,128)(2,1)} %constant.8.clone.forward_ref) | copy-start | bytes 1179652
  0.6 21.9 %copy-start.3 = (f32[17,2,8,128]{3,2,1,0:T(8,128)S(1)}, f32[17,2,8,128]{3,2,1,0:T(8,128)}, u32[]{:S(2)}) copy-start(f32[17,2,8,128]{3,2,1,0:T(8,128)} %constant.10.clone.twiddle_ref) | copy-start | bytes 417796
  1.9 20.6 %copy-start = (bf16[768,256]{1,0:T(8,128)(2,1)S(1)}, bf16[768,256]{1,0:T(8,128)(2,1)}, u32[]{:S(2)}) copy-start(bf16[768,256]{1,0:T(8,128)(2,1)} %constant.9.clone.inverse_ref) | copy-start | bytes 1179652
  1.9 20.6 %copy-start.2 = (f32[17,2,8,128]{3,2,1,0:T(8,128)S(1)}, f32[17,2,8,128]{3,2,1,0:T(8,128)}, u32[]{:S(2)}) copy-start(f32[17,2,8,128]{3,2,1,0:T(8,128)} %constant.11.clone.rowfix_ref) | copy-start | bytes 417796
  23.4 5.1 %collective-permute-start = (f32[64,128]{1,0:T(8,128)S(1)}, f32[64,128]{1,0:T(8,128)S(1)}, u32[]{:S(2)}, u32[]{:S(2)}) collective-permute-start(f32[64,128]{1,0:T(8,128)S(1)} %get-tuple-element.10), channel_id=1, source_target_pairs={{0,193},{1,64},{64,1},{65,128},{128,65},{129,192},{192,129},{193,0... | collective-permute-start | bytes 98312 | tf_op jit(solution)/shard_map/ppermute | solution.py:316
  28.4 6.3 %collective-permute-start.1 = (f32[64,128]{1,0:T(8,128)S(1)}, f32[64,128]{1,0:T(8,128)S(1)}, u32[]{:S(2)}, u32[]{:S(2)}) collective-permute-start(f32[64,128]{1,0:T(8,128)S(1)} %add.6), channel_id=1, source_target_pairs={{0,65},{1,192},{64,129},{65,0},{128,193},{129,64},{192,1},{193,128... | collective-permute-start | bytes 98312 | tf_op jit(solution)/shard_map/ppermute | solution.py:316
  34.8 15.4 %copy-start.4 = (f32[1,128,256]{2,1,0:T(8,128)S(1)}, f32[1,128,256]{2,1,0:T(8,128)}, u32[]{:S(2)}) copy-start(f32[1,128,256]{2,1,0:T(8,128)} %param.9) | copy-start | bytes 393220
  34.8 15.3 %copy-start.5 = (f32[1,128,256]{2,1,0:T(8,128)S(1)}, f32[1,128,256]{2,1,0:T(8,128)}, u32[]{:S(2)}) copy-start(f32[1,128,256]{2,1,0:T(8,128)} %param.10) | copy-start | bytes 393220
  34.8 15.3 %copy-start.6 = (f32[1,128,256]{2,1,0:T(8,128)S(1)}, f32[1,128,256]{2,1,0:T(8,128)}, u32[]{:S(2)}) copy-start(f32[1,128,256]{2,1,0:T(8,128)} %param.12) | copy-start | bytes 393220

commit v6 on v5

--- a/solution.py
+++ b/solution.py
@@ -12,13 +12,13 @@
 ORDERS = ((3, 2, 1, 0), (1, 0, 3, 2))
 STEPS = [
     [
-        (2 * zh + core, 2 * ORDERS[(step + core + zh + 0) % 2][zh] + 1 - core)
+        (2 * zh + core, 2 * ORDERS[(step + core + zh) % 2][zh] + 1 - core)
         for zh in range(4)
         for core in range(2)
     ]
     for step in range(2)
 ]
-FAR = ("y", "x", "zl", "core")
+FAR = ("zl", "x", "y", "core")
 BLOCKS = 17
 CLASSES = [0, 16, 8, 4, 20] + [8 * j + 2 for j in range(4)] + [4 * j + 1 for j in range(8)]
 VMEM = pl.BlockSpec(memory_space=pltpu.VMEM)
@@ -178,6 +178,10 @@
         out_ref[pl.ds(core * 9 + 8, 32, stride=18), :] = filter_ref[core] * (1.0 / 64)
 
 
+def place(y, c):
+    return (c // 2 % 2) * 32 + (c // 4) * 8 + y * 2 + c % 2
+
+
 def spectrum_rows(blocks, scratch, base, sign, twiddle_ref, rowfix_ref):
     for index, value in enumerate(blocks_forward(blocks)):
         fix = (rowfix_ref[index, 0], rowfix_ref[index, 1])
@@ -206,7 +210,7 @@
 def forward_kernel(signal_ref, forward_ref, inverse_ref, twiddle_ref, rowfix_ref, spec_ref, part_ref, raw):
     sign = half_sign()
     for y in range(4):
-        blocks = [signal_ref[(y * 16 + c) * 9 : (y * 16 + c) * 9 + 8, :] for c in range(16)]
+        blocks = [signal_ref[place(y, c) * 9 : place(y, c) * 9 + 8, :] for c in range(16)]
         spectrum_rows(blocks, raw, y * 136, sign, twiddle_ref, rowfix_ref)
         multiply(raw, spec_ref, forward_ref, y * 136)
     for index in range(BLOCKS):
@@ -231,10 +235,10 @@
     sign = half_sign()
     for y in range(4):
         at = (y // 2) * 4 + y % 2
-        for c in range(0, 16, 8):
-            rows = signal_ref[pl.ds((y * 16 + c) * 9 + 8, 8, stride=9), :]
-            taps[pl.ds(c * 8 + at, 8, stride=8), :] = rows
-            taps[pl.ds(c * 8 + at + 2, 8, stride=8), :] = rows
+        for c in range(4):
+            rows = signal_ref[pl.ds(place(y, c) * 9 + 8, 4, stride=72), :]
+            taps[pl.ds(c * 8 + at, 4, stride=32), :] = rows
+            taps[pl.ds(c * 8 + at + 2, 4, stride=32), :] = rows
     spectrum_rows([taps[c * 8 : c * 8 + 8, :] for c in range(16)], raw, 544, sign, twiddle_ref, rowfix_ref)
     multiply(raw, spec, forward_ref, 544)
     rows = lax.broadcasted_iota(jnp.int32, (8, 128), 0)
@@ -250,7 +254,7 @@
         multiply(raw, spec, inverse_ref, y * 136)
         blocks = blocks_of(spec, y * 136, sign, twiddle_ref, rowfix_ref)
         for c in range(16):
-            at = (y * 16 + c) * 12
+            at = place(y, c) * 12
             out_ref[at : at + 8, :] = blocks[c]
 
 
@@ -263,7 +267,7 @@
             pair = pair + more[c * 4 : c * 4 + 8, :]
         pair = pair * (1.0 / 64)
         for y in range(4):
-            at = (y * 16 + c) * 12
+            at = place(y, c) * 12
             out_ref[at + 8 : at + 12, :] = pair[0:4, :]
             out_ref[at + 20 : at + 24, :] = pair[4:8, :]
 

time: 51.2 us -> 50.5 us (0.986)
  blocking collectives: 35.9 us -> 35.2 us
    all_to_all x2, blocking collectives: 35.9 us -> 35.2 us  [exchange(): return lax.all_to_all(array, axes, split_axis=0, concat_axis=0, tiled=True)]
  transfers between devices with their start and end apart: 2 -> 2, of which waited for: 2 -> 2; matrix products, arithmetic and copies ran while one was open for 0% -> 0% of each run, Pallas kernels for 1% -> 2%
where the time goes in v6:
time: 50.5 us; the launch traced here: 50.3 us
  blocking collectives  35.2 us (70%)
  starting transfers between devices  8.21 us (16%)
  Pallas kernels  3.7 us (7%)
  waiting for transfers between devices  2.43 us (5%)
  between operations  0.73 us (1%)
    all_to_all x2, blocking collectives, exchange(): return lax.all_to_all(array, axes, split_axis=0, concat_axis=0, tiled=True)  35.2 us
    ppermute x2, starting transfers between devices, on_device(): part = part + lax.ppermute(part, ('zh', 'core'), pairs)  8.21 us
    ppermute x2, waiting for transfers between devices, on_device(): part = part + lax.ppermute(part, ('zh', 'core'), pairs)  2.43 us
    pallas_call x1, Pallas kernels, on_device(): call(pack_kernel, [(576, 128)], 5, [(128, 256)] * 4 + [(2, 32, 128)], cop...  1.23 us
  transfers between devices with their start and end apart: 2, of which 2 were waited for; matrix products, arithmetic and copies ran while one was open for 0% of the time, Pallas kernels for 2%

profile of v6, /device:TPU:1, one launch (start us, length us, event | category | flops | bytes accessed | tf_op | source)
XLA Modules:
  0.0 50.3 jit_solution(17147136648095186973)
XLA Ops:
  0.6 0.0 copy-start.1
  0.6 0.0 copy-start.3
  0.7 1.2 %shard_map.120 = f32[576,128]{1,0:T(8,128)S(1)} custom-call(f32[128,256]{1,0:T(8,128)} %bitcast.16, f32[128,256]{1,0:T(8,128)} %bitcast.18, f32[128,256]{1,0:T(8,128)} %bitcast.22, f32[128,256]{1,0:T(8,128)} %bitcast.20, f32[128,256]{1,0:T(8,128)} %filter_hbm.1), custom_call_target="tpu_custom_call" | custom-call | tf_op jit(solution)/shard_map/pallas_call | solution.py:312
  1.9 0.0 copy-start
  1.9 0.0 copy-start.2
  1.9 20.3 %all_to_all.10 = f32[64,1,1152]{2,1,0:T(1,128)S(1)} all-to-all(f32[64,1,1152]{2,1,0:T(1,128)S(1)} %bitcast.15), channel_id=1, replica_groups=mesh['zh'=4,'y'=4,'x'=4,'zl'=2,'core'=2] {'zl','x','y','core'}, dimensions={0} | all-to-all | bytes 589824 | tf_op jit(solution)/shard_map/all_to_all | solution.py:305
  22.2 0.0 copy-done.1
  22.2 0.0 copy-done.3
  22.2 0.0 copy-done
  22.2 0.0 copy-done.2
  22.3 0.8 %shard_map.121 = (f32[544,256]{1,0:T(8,128)S(1)}, f32[64,128]{1,0:T(8,128)S(1)}) custom-call(f32[576,128]{1,0:T(8,128)S(1)} %bitcast.11, bf16[768,256]{1,0:T(8,128)(2,1)S(1)} %copy-done.1, bf16[768,256]{1,0:T(8,128)(2,1)S(1)} %copy-done, f32[17,2,8,128]{3,2,1,0:T(8,128)S(1)} %copy-done.3, f32[17,2,8,128]{3,2,1,0:T(8,128)S(1)} %copy-done.2), custom_call_target="tpu_custom_call" | custom-call | tf_op jit(solution)/shard_map/pallas_call | solution.py:316
  23.1 3.4 %collective-permute-start = (f32[64,128]{1,0:T(8,128)S(1)}, f32[64,128]{1,0:T(8,128)S(1)}, u32[]{:S(2)}, u32[]{:S(2)}) collective-permute-start(f32[64,128]{1,0:T(8,128)S(1)} %get-tuple-element.10), channel_id=1, source_target_pairs={{0,193},{1,64},{64,1},{65,128},{128,65},{129,192},{192,129},{193,0... | collective-permute-start | bytes 98312 | tf_op jit(solution)/shard_map/ppermute | solution.py:320
  26.4 1.6 %collective-permute-done = f32[64,128]{1,0:T(8,128)S(1)} collective-permute-done((f32[64,128]{1,0:T(8,128)S(1)}, f32[64,128]{1,0:T(8,128)S(1)}, u32[]{:S(2)}, u32[]{:S(2)}) %collective-permute-start) | collective-permute-done | bytes 32800 | tf_op jit(solution)/shard_map/ppermute | solution.py:320
  28.0 4.9 %collective-permute-start.1 = (f32[64,128]{1,0:T(8,128)S(1)}, f32[64,128]{1,0:T(8,128)S(1)}, u32[]{:S(2)}, u32[]{:S(2)}) collective-permute-start(f32[64,128]{1,0:T(8,128)S(1)} %add.6), channel_id=1, source_target_pairs={{0,65},{1,192},{64,129},{65,0},{128,193},{129,64},{192,1},{193,128... | collective-permute-start | bytes 98312 | tf_op jit(solution)/shard_map/ppermute | solution.py:320
  32.9 0.8 %shard_map.122.refs_0_ = f32[768,128]{1,0:T(8,128)S(1)} custom-call(f32[576,128]{1,0:T(8,128)S(1)} %bitcast.12, f32[544,256]{1,0:T(8,128)S(1)} %get-tuple-element.11.spec_ref, bf16[768,256]{1,0:T(8,128)(2,1)S(1)} %copy-done.1, bf16[768,256]{1,0:T(8,128)(2,1)S(1)} %copy-done, f32[17,2,8,128]{3,2,1,0:T(8,128)S(1)} %copy-done.3, f32[17,2,8,128]{3,2,1,0:T(8,128)S(1)} %copy-done.2), custom_call_target="tpu_custom_call" | custom-call | tf_op jit(solution)/shard_map/pallas_call | solution.py:321
  33.6 0.8 %collective-permute-done.1 = f32[64,128]{1,0:T(8,128)S(1)} collective-permute-done((f32[64,128]{1,0:T(8,128)S(1)}, f32[64,128]{1,0:T(8,128)S(1)}, u32[]{:S(2)}, u32[]{:S(2)}) %collective-permute-start.1) | collective-permute-done | bytes 32800 | tf_op jit(solution)/shard_map/ppermute | solution.py:320
  34.5 0.0 copy-start.4
  34.5 0.0 copy-start.5
  34.6 0.0 copy-start.6
  34.6 14.8 %all_to_all.11 = f32[64,1,1536]{2,1,0:T(1,128)S(1)} all-to-all(f32[64,1,1536]{2,1,0:T(1,128)S(1)} %bitcast.14), channel_id=1, replica_groups=mesh['zh'=4,'y'=4,'x'=4,'zl'=2,'core'=2] {'zl','x','y','core'}, dimensions={0} | all-to-all | bytes 786432 | tf_op jit(solution)/shard_map/all_to_all | solution.py:305
  49.4 0.0 copy-done.4
  49.4 0.0 copy-done.5
  49.4 0.0 copy-done.6
  49.4 0.9 %shard_map.124 = (f32[128,256]{1,0:T(8,128)}, f32[128,256]{1,0:T(8,128)}, f32[128,256]{1,0:T(8,128)}, f32[128,256]{1,0:T(8,128)}) custom-call(f32[768,128]{1,0:T(8,128)S(1)} %bitcast.13, f32[128,256]{1,0:T(8,128)S(1)} %bitcast.17, f32[128,256]{1,0:T(8,128)S(1)} %bitcast.19, f32[128,256]{1,0:T(8,128)S(1)} %bitcast.21), custom_call_target="tpu_custom_call" | custom-call | tf_op jit(solution)/shard_map/pallas_call | solution.py:327
  (3 shorter events, 0.0 us)
Async XLA Ops:
  0.6 21.6 %copy-start.1 = (bf16[768,256]{1,0:T(8,128)(2,1)S(1)}, bf16[768,256]{1,0:T(8,128)(2,1)}, u32[]{:S(2)}) copy-start(bf16[768,256]{1,0:T(8,128)(2,1)} %constant.8.clone.forward_ref) | copy-start | bytes 1179652
  0.6 21.6 %copy-start.3 = (f32[17,2,8,128]{3,2,1,0:T(8,128)S(1)}, f32[17,2,8,128]{3,2,1,0:T(8,128)}, u32[]{:S(2)}) copy-start(f32[17,2,8,128]{3,2,1,0:T(8,128)} %constant.10.clone.twiddle_ref) | copy-start | bytes 417796
  1.9 20.3 %copy-start = (bf16[768,256]{1,0:T(8,128)(2,1)S(1)}, bf16[768,256]{1,0:T(8,128)(2,1)}, u32[]{:S(2)}) copy-start(bf16[768,256]{1,0:T(8,128)(2,1)} %constant.9.clone.inverse_ref) | copy-start | bytes 1179652
  1.9 20.3 %copy-start.2 = (f32[17,2,8,128]{3,2,1,0:T(8,128)S(1)}, f32[17,2,8,128]{3,2,1,0:T(8,128)}, u32[]{:S(2)}) copy-start(f32[17,2,8,128]{3,2,1,0:T(8,128)} %constant.11.clone.rowfix_ref) | copy-start | bytes 417796
  23.1 5.0 %collective-permute-start = (f32[64,128]{1,0:T(8,128)S(1)}, f32[64,128]{1,0:T(8,128)S(1)}, u32[]{:S(2)}, u32[]{:S(2)}) collective-permute-start(f32[64,128]{1,0:T(8,128)S(1)} %get-tuple-element.10), channel_id=1, source_target_pairs={{0,193},{1,64},{64,1},{65,128},{128,65},{129,192},{192,129},{193,0... | collective-permute-start | bytes 98312 | tf_op jit(solution)/shard_map/ppermute | solution.py:320
  28.0 6.5 %collective-permute-start.1 = (f32[64,128]{1,0:T(8,128)S(1)}, f32[64,128]{1,0:T(8,128)S(1)}, u32[]{:S(2)}, u32[]{:S(2)}) collective-permute-start(f32[64,128]{1,0:T(8,128)S(1)} %add.6), channel_id=1, source_target_pairs={{0,65},{1,192},{64,129},{65,0},{128,193},{129,64},{192,1},{193,128... | collective-permute-start | bytes 98312 | tf_op jit(solution)/shard_map/ppermute | solution.py:320
  34.5 14.9 %copy-start.4 = (f32[1,128,256]{2,1,0:T(8,128)S(1)}, f32[1,128,256]{2,1,0:T(8,128)}, u32[]{:S(2)}) copy-start(f32[1,128,256]{2,1,0:T(8,128)} %param.9) | copy-start | bytes 393220
  34.5 14.9 %copy-start.5 = (f32[1,128,256]{2,1,0:T(8,128)S(1)}, f32[1,128,256]{2,1,0:T(8,128)}, u32[]{:S(2)}) copy-start(f32[1,128,256]{2,1,0:T(8,128)} %param.10) | copy-start | bytes 393220
  34.6 14.9 %copy-start.6 = (f32[1,128,256]{2,1,0:T(8,128)S(1)}, f32[1,128,256]{2,1,0:T(8,128)}, u32[]{:S(2)}) copy-start(f32[1,128,256]{2,1,0:T(8,128)} %param.12) | copy-start | bytes 393220

commit v7 on v6

--- a/solution.py
+++ b/solution.py
@@ -144,7 +144,7 @@
     return odd * 64, (1 - odd) * 64
 
 
-def pack_kernel(value_hbm, key_hbm, query_hbm, cot_hbm, filter_hbm, out_ref, value_ref, key_ref, query_ref, cot_ref, filter_ref, sems):
+def pack_kernel(value_hbm, key_hbm, query_hbm, cot_hbm, filter_hbm, out_ref, value_ref, key_ref, cot_ref, query_ref, filter_ref, sems):
     copies = [
         pltpu.make_async_copy(value_hbm, value_ref, sems.at[0]),
         pltpu.make_async_copy(key_hbm, key_ref, sems.at[1]),
@@ -309,9 +309,8 @@
     value_in, key_in, query_in, cotangent = value_in[0], key_in[0], query_in[0], cotangent[0]
     forward, inverse, twiddle, rowfix = [jnp.asarray(table) for table in tables()]
     pinned = [pltpu.with_memory_space_constraint(a, pltpu.HBM) for a in (value_in, key_in, query_in, cotangent, filter_param)]
-    (message,) = call(pack_kernel, [(576, 128)], 5, [(128, 256)] * 4 + [(2, 32, 128)], copies=6)(
-        *pinned
-    )
+    shape = (128, 256)
+    message, value, key, cot = call(pack_kernel, [(576, 128)] + [shape] * 3, 5, [shape, (2, 32, 128)], copies=6)(*pinned)
     signal = exchange(message.reshape(64, 1, 1152), FAR).reshape(576, 128)
     spec, part = call(forward_kernel, [(544, 256), (64, 128)], 5, [(680, 256)])(
         signal, forward, inverse, twiddle, rowfix
@@ -323,10 +322,7 @@
     )
     (message,) = call(filter_kernel, [(768, 128)], 2)(part, message)
     signal = exchange(message.reshape(64, 1, 1536), FAR).reshape(768, 128)
-    shape = (128, 256)
-    query_grad, key_grad, value_grad, filter_grad = call(unpack_kernel, [shape] * 4, 4)(
-        signal, value_in, key_in, cotangent
-    )
+    query_grad, key_grad, value_grad, filter_grad = call(unpack_kernel, [shape] * 4, 4)(signal, value, key, cot)
     return query_grad[None], key_grad[None], value_grad[None], filter_grad
 
 

time: 50.5 us -> 50.3 us (level)
  no operation moved by 1% of the time
where the time goes in v7:
time: 50.3 us; the launch traced here: 50.1 us
  blocking collectives  35 us (70%)
  starting transfers between devices  8.21 us (16%)
  Pallas kernels  3.7 us (7%)
  waiting for transfers between devices  2.43 us (5%)
  between operations  0.71 us (1%)
    all_to_all x2, blocking collectives, exchange(): return lax.all_to_all(array, axes, split_axis=0, concat_axis=0, tiled=True)  35 us
    ppermute x2, starting transfers between devices, on_device(): part = part + lax.ppermute(part, ('zh', 'core'), pairs)  8.21 us
    ppermute x2, waiting for transfers between devices, on_device(): part = part + lax.ppermute(part, ('zh', 'core'), pairs)  2.43 us
    pallas_call x1, Pallas kernels, on_device(): call(pack_kernel, [(576, 128)] + [shape] * 3, 5, [shape, (2, 32, 128)], c...  1.22 us
  transfers between devices with their start and end apart: 2, of which 2 were waited for; matrix products, arithmetic and copies ran while one was open for 0% of the time, Pallas kernels for 2%

profile of v7, /device:TPU:1, one launch (start us, length us, event | category | flops | bytes accessed | tf_op | source)
XLA Modules:
  0.0 50.1 jit_solution(9811487626417048319)
XLA Ops:
  0.6 0.0 copy-start.1
  0.6 0.0 copy-start.3
  0.7 1.2 %shard_map.120 = (f32[576,128]{1,0:T(8,128)S(1)}, f32[128,256]{1,0:T(8,128)S(1)}, f32[128,256]{1,0:T(8,128)S(1)}, f32[128,256]{1,0:T(8,128)S(1)}) custom-call(f32[128,256]{1,0:T(8,128)} %bitcast.16, f32[128,256]{1,0:T(8,128)} %bitcast.17, f32[128,256]{1,0:T(8,128)} %bitcast.18, f32[128,256]{1,0:T(8,128)} %bitcast.19, f32[128,256]{1,0:T(8,128)} %filter_hbm.1), custom_call_target="tpu_custom_call" | custom-call | tf_op jit(solution)/shard_map/pallas_call | solution.py:313
  1.9 0.0 copy-start
  1.9 0.0 copy-start.2
  1.9 20.3 %all_to_all.10 = f32[64,1,1152]{2,1,0:T(1,128)S(1)} all-to-all(f32[64,1,1152]{2,1,0:T(1,128)S(1)} %bitcast.15), channel_id=1, replica_groups=mesh['zh'=4,'y'=4,'x'=4,'zl'=2,'core'=2] {'zl','x','y','core'}, dimensions={0} | all-to-all | bytes 589824 | tf_op jit(solution)/shard_map/all_to_all | solution.py:305
  22.2 0.0 copy-done.1
  22.2 0.0 copy-done.3
  22.2 0.0 copy-done
  22.2 0.0 copy-done.2
  22.2 0.8 %shard_map.121 = (f32[544,256]{1,0:T(8,128)S(1)}, f32[64,128]{1,0:T(8,128)S(1)}) custom-call(f32[576,128]{1,0:T(8,128)S(1)} %bitcast.11, bf16[768,256]{1,0:T(8,128)(2,1)S(1)} %copy-done.1, bf16[768,256]{1,0:T(8,128)(2,1)S(1)} %copy-done, f32[17,2,8,128]{3,2,1,0:T(8,128)S(1)} %copy-done.3, f32[17,2,8,128]{3,2,1,0:T(8,128)S(1)} %copy-done.2), custom_call_target="tpu_custom_call" | custom-call | tf_op jit(solution)/shard_map/pallas_call | solution.py:315
  23.1 3.4 %collective-permute-start = (f32[64,128]{1,0:T(8,128)S(1)}, f32[64,128]{1,0:T(8,128)S(1)}, u32[]{:S(2)}, u32[]{:S(2)}) collective-permute-start(f32[64,128]{1,0:T(8,128)S(1)} %get-tuple-element.15), channel_id=1, source_target_pairs={{0,193},{1,64},{64,1},{65,128},{128,65},{129,192},{192,129},{193,0... | collective-permute-start | bytes 98312 | tf_op jit(solution)/shard_map/ppermute | solution.py:319
  26.4 1.6 %collective-permute-done = f32[64,128]{1,0:T(8,128)S(1)} collective-permute-done((f32[64,128]{1,0:T(8,128)S(1)}, f32[64,128]{1,0:T(8,128)S(1)}, u32[]{:S(2)}, u32[]{:S(2)}) %collective-permute-start) | collective-permute-done | bytes 32800 | tf_op jit(solution)/shard_map/ppermute | solution.py:319
  28.0 4.9 %collective-permute-start.1 = (f32[64,128]{1,0:T(8,128)S(1)}, f32[64,128]{1,0:T(8,128)S(1)}, u32[]{:S(2)}, u32[]{:S(2)}) collective-permute-start(f32[64,128]{1,0:T(8,128)S(1)} %add.6), channel_id=1, source_target_pairs={{0,65},{1,192},{64,129},{65,0},{128,193},{129,64},{192,1},{193,128... | collective-permute-start | bytes 98312 | tf_op jit(solution)/shard_map/ppermute | solution.py:319
  32.9 0.8 %shard_map.122.refs_0_ = f32[768,128]{1,0:T(8,128)S(1)} custom-call(f32[576,128]{1,0:T(8,128)S(1)} %bitcast.12, f32[544,256]{1,0:T(8,128)S(1)} %get-tuple-element.16.spec_ref, bf16[768,256]{1,0:T(8,128)(2,1)S(1)} %copy-done.1, bf16[768,256]{1,0:T(8,128)(2,1)S(1)} %copy-done, f32[17,2,8,128]{3,2,1,0:T(8,128)S(1)} %copy-done.3, f32[17,2,8,128]{3,2,1,0:T(8,128)S(1)} %copy-done.2), custom_call_target="tpu_custom_call" | custom-call | tf_op jit(solution)/shard_map/pallas_call | solution.py:320
  33.6 0.8 %collective-permute-done.1 = f32[64,128]{1,0:T(8,128)S(1)} collective-permute-done((f32[64,128]{1,0:T(8,128)S(1)}, f32[64,128]{1,0:T(8,128)S(1)}, u32[]{:S(2)}, u32[]{:S(2)}) %collective-permute-start.1) | collective-permute-done | bytes 32800 | tf_op jit(solution)/shard_map/ppermute | solution.py:319
  34.5 14.7 %all_to_all.11 = f32[64,1,1536]{2,1,0:T(1,128)S(1)} all-to-all(f32[64,1,1536]{2,1,0:T(1,128)S(1)} %bitcast.14), channel_id=1, replica_groups=mesh['zh'=4,'y'=4,'x'=4,'zl'=2,'core'=2] {'zl','x','y','core'}, dimensions={0} | all-to-all | bytes 786432 | tf_op jit(solution)/shard_map/all_to_all | solution.py:305
  49.2 0.9 %shard_map.124 = (f32[128,256]{1,0:T(8,128)}, f32[128,256]{1,0:T(8,128)}, f32[128,256]{1,0:T(8,128)}, f32[128,256]{1,0:T(8,128)}) custom-call(f32[768,128]{1,0:T(8,128)S(1)} %bitcast.13, f32[128,256]{1,0:T(8,128)S(1)} %get-tuple-element.17.value_ref, f32[128,256]{1,0:T(8,128)S(1)} %get-tuple-element.18.key_ref, f32[128,256]{1,0:T(8,128)S(1)} %get-tuple-element.19.cot_ref), custom_call_target="tpu_custom_call" | custom-call | tf_op jit(solution)/shard_map/pallas_call | solution.py:325
  (3 shorter events, 0.0 us)
Async XLA Ops:
  0.6 21.6 %copy-start.1 = (bf16[768,256]{1,0:T(8,128)(2,1)S(1)}, bf16[768,256]{1,0:T(8,128)(2,1)}, u32[]{:S(2)}) copy-start(bf16[768,256]{1,0:T(8,128)(2,1)} %constant.8.clone.forward_ref) | copy-start | bytes 1179652
  0.6 21.6 %copy-start.3 = (f32[17,2,8,128]{3,2,1,0:T(8,128)S(1)}, f32[17,2,8,128]{3,2,1,0:T(8,128)}, u32[]{:S(2)}) copy-start(f32[17,2,8,128]{3,2,1,0:T(8,128)} %constant.10.clone.twiddle_ref) | copy-start | bytes 417796
  1.9 20.3 %copy-start = (bf16[768,256]{1,0:T(8,128)(2,1)S(1)}, bf16[768,256]{1,0:T(8,128)(2,1)}, u32[]{:S(2)}) copy-start(bf16[768,256]{1,0:T(8,128)(2,1)} %constant.9.clone.inverse_ref) | copy-start | bytes 1179652
  1.9 20.3 %copy-start.2 = (f32[17,2,8,128]{3,2,1,0:T(8,128)S(1)}, f32[17,2,8,128]{3,2,1,0:T(8,128)}, u32[]{:S(2)}) copy-start(f32[17,2,8,128]{3,2,1,0:T(8,128)} %constant.11.clone.rowfix_ref) | copy-start | bytes 417796
  23.1 5.0 %collective-permute-start = (f32[64,128]{1,0:T(8,128)S(1)}, f32[64,128]{1,0:T(8,128)S(1)}, u32[]{:S(2)}, u32[]{:S(2)}) collective-permute-start(f32[64,128]{1,0:T(8,128)S(1)} %get-tuple-element.15), channel_id=1, source_target_pairs={{0,193},{1,64},{64,1},{65,128},{128,65},{129,192},{192,129},{193,0... | collective-permute-start | bytes 98312 | tf_op jit(solution)/shard_map/ppermute | solution.py:319
  28.0 6.5 %collective-permute-start.1 = (f32[64,128]{1,0:T(8,128)S(1)}, f32[64,128]{1,0:T(8,128)S(1)}, u32[]{:S(2)}, u32[]{:S(2)}) collective-permute-start(f32[64,128]{1,0:T(8,128)S(1)} %add.6), channel_id=1, source_target_pairs={{0,65},{1,192},{64,129},{65,0},{128,193},{129,64},{192,1},{193,128... | collective-permute-start | bytes 98312 | tf_op jit(solution)/shard_map/ppermute | solution.py:319

commit v8 on v7

--- a/solution.py
+++ b/solution.py
@@ -37,7 +37,7 @@
     def split(table):
         high = table.astype(np.float32).astype(jnp.bfloat16)
         low = (table - high.astype(np.float64)).astype(np.float32).astype(jnp.bfloat16)
-        return np.concatenate([high, high, low], 0)
+        return np.concatenate([high, low], 0)
 
     row_half = np.arange(8) // 4
     twiddle = np.zeros((BLOCKS, 2, 8, 128), np.float32)
@@ -132,11 +132,14 @@
 
 
 def multiply(source, target, table, start):
+    high_table, low_table = table[0:256, :], table[256:512, :]
     block = source[start : start + 136, :]
     high = block.astype(jnp.bfloat16)
     low = (block - high.astype(jnp.float32)).astype(jnp.bfloat16)
-    parts = jnp.concatenate([high, low, high], 1)
-    target[start : start + 136, :] = jnp.dot(parts, table[...], preferred_element_type=jnp.float32)
+    total = jnp.dot(high, low_table, preferred_element_type=jnp.float32)
+    total += jnp.dot(low, high_table, preferred_element_type=jnp.float32)
+    total += jnp.dot(high, high_table, preferred_element_type=jnp.float32)
+    target[start : start + 136, :] = total
 
 
 def channel_bases():

time: 50.3 us -> 50.3 us (level)
  no operation moved by 1% of the time
where the time goes in v8:
time: 50.3 us; the launch traced here: 50.1 us
  blocking collectives  35 us (70%)
  starting transfers between devices  8.21 us (16%)
  Pallas kernels  3.67 us (7%)
  waiting for transfers between devices  2.45 us (5%)
  between operations  0.71 us (1%)
    all_to_all x2, blocking collectives, exchange(): return lax.all_to_all(array, axes, split_axis=0, concat_axis=0, tiled=True)  35 us
    ppermute x2, starting transfers between devices, on_device(): part = part + lax.ppermute(part, ('zh', 'core'), pairs)  8.21 us
    ppermute x2, waiting for transfers between devices, on_device(): part = part + lax.ppermute(part, ('zh', 'core'), pairs)  2.45 us
    pallas_call x1, Pallas kernels, on_device(): call(pack_kernel, [(576, 128)] + [shape] * 3, 5, [shape, (2, 32, 128)], c...  1.21 us
  transfers between devices with their start and end apart: 2, of which 2 were waited for; matrix products, arithmetic and copies ran while one was open for 0% of the time, Pallas kernels for 2%

profile of v8, /device:TPU:1, one launch (start us, length us, event | category | flops | bytes accessed | tf_op | source)
XLA Modules:
  0.0 50.1 jit_solution(10070663297908216154)
XLA Ops:
  0.6 0.0 copy-start.2
  0.6 0.0 copy-start.3
  0.7 1.2 %shard_map.120 = (f32[576,128]{1,0:T(8,128)S(1)}, f32[128,256]{1,0:T(8,128)S(1)}, f32[128,256]{1,0:T(8,128)S(1)}, f32[128,256]{1,0:T(8,128)S(1)}) custom-call(f32[128,256]{1,0:T(8,128)} %bitcast.16, f32[128,256]{1,0:T(8,128)} %bitcast.17, f32[128,256]{1,0:T(8,128)} %bitcast.18, f32[128,256]{1,0:T(8,128)} %bitcast.19, f32[128,256]{1,0:T(8,128)} %filter_hbm.1), custom_call_target="tpu_custom_call" | custom-call | tf_op jit(solution)/shard_map/pallas_call | solution.py:316
  1.9 0.0 copy-start
  1.9 0.0 copy-start.1
  1.9 20.3 %all_to_all.10 = f32[64,1,1152]{2,1,0:T(1,128)S(1)} all-to-all(f32[64,1,1152]{2,1,0:T(1,128)S(1)} %bitcast.15), channel_id=1, replica_groups=mesh['zh'=4,'y'=4,'x'=4,'zl'=2,'core'=2] {'zl','x','y','core'}, dimensions={0} | all-to-all | bytes 589824 | tf_op jit(solution)/shard_map/all_to_all | solution.py:308
  22.2 0.0 copy-done.2
  22.2 0.0 copy-done.3
  22.2 0.0 copy-done
  22.2 0.0 copy-done.1
  22.2 0.8 %shard_map.121 = (f32[544,256]{1,0:T(8,128)S(1)}, f32[64,128]{1,0:T(8,128)S(1)}) custom-call(f32[576,128]{1,0:T(8,128)S(1)} %bitcast.11, bf16[512,256]{1,0:T(8,128)(2,1)S(1)} %copy-done.1, bf16[512,256]{1,0:T(8,128)(2,1)S(1)} %copy-done, f32[17,2,8,128]{3,2,1,0:T(8,128)S(1)} %copy-done.3, f32[17,2,8,128]{3,2,1,0:T(8,128)S(1)} %copy-done.2), custom_call_target="tpu_custom_call" | custom-call | tf_op jit(solution)/shard_map/pallas_call | solution.py:318
  23.0 3.4 %collective-permute-start = (f32[64,128]{1,0:T(8,128)S(1)}, f32[64,128]{1,0:T(8,128)S(1)}, u32[]{:S(2)}, u32[]{:S(2)}) collective-permute-start(f32[64,128]{1,0:T(8,128)S(1)} %get-tuple-element.15), channel_id=1, source_target_pairs={{0,193},{1,64},{64,1},{65,128},{128,65},{129,192},{192,129},{193,0... | collective-permute-start | bytes 98312 | tf_op jit(solution)/shard_map/ppermute | solution.py:322
  26.4 1.6 %collective-permute-done = f32[64,128]{1,0:T(8,128)S(1)} collective-permute-done((f32[64,128]{1,0:T(8,128)S(1)}, f32[64,128]{1,0:T(8,128)S(1)}, u32[]{:S(2)}, u32[]{:S(2)}) %collective-permute-start) | collective-permute-done | bytes 32800 | tf_op jit(solution)/shard_map/ppermute | solution.py:322
  28.0 4.9 %collective-permute-start.1 = (f32[64,128]{1,0:T(8,128)S(1)}, f32[64,128]{1,0:T(8,128)S(1)}, u32[]{:S(2)}, u32[]{:S(2)}) collective-permute-start(f32[64,128]{1,0:T(8,128)S(1)} %add.6), channel_id=1, source_target_pairs={{0,65},{1,192},{64,129},{65,0},{128,193},{129,64},{192,1},{193,128... | collective-permute-start | bytes 98312 | tf_op jit(solution)/shard_map/ppermute | solution.py:322
  32.9 0.8 %shard_map.122.refs_0_ = f32[768,128]{1,0:T(8,128)S(1)} custom-call(f32[576,128]{1,0:T(8,128)S(1)} %bitcast.12, f32[544,256]{1,0:T(8,128)S(1)} %get-tuple-element.16.spec_ref, bf16[512,256]{1,0:T(8,128)(2,1)S(1)} %copy-done.1, bf16[512,256]{1,0:T(8,128)(2,1)S(1)} %copy-done, f32[17,2,8,128]{3,2,1,0:T(8,128)S(1)} %copy-done.3, f32[17,2,8,128]{3,2,1,0:T(8,128)S(1)} %copy-done.2), custom_call_target="tpu_custom_call" | custom-call | tf_op jit(solution)/shard_map/pallas_call | solution.py:323
  33.6 0.8 %collective-permute-done.1 = f32[64,128]{1,0:T(8,128)S(1)} collective-permute-done((f32[64,128]{1,0:T(8,128)S(1)}, f32[64,128]{1,0:T(8,128)S(1)}, u32[]{:S(2)}, u32[]{:S(2)}) %collective-permute-start.1) | collective-permute-done | bytes 32800 | tf_op jit(solution)/shard_map/ppermute | solution.py:322
  34.5 14.7 %all_to_all.11 = f32[64,1,1536]{2,1,0:T(1,128)S(1)} all-to-all(f32[64,1,1536]{2,1,0:T(1,128)S(1)} %bitcast.14), channel_id=1, replica_groups=mesh['zh'=4,'y'=4,'x'=4,'zl'=2,'core'=2] {'zl','x','y','core'}, dimensions={0} | all-to-all | bytes 786432 | tf_op jit(solution)/shard_map/all_to_all | solution.py:308
  49.2 0.9 %shard_map.124 = (f32[128,256]{1,0:T(8,128)}, f32[128,256]{1,0:T(8,128)}, f32[128,256]{1,0:T(8,128)}, f32[128,256]{1,0:T(8,128)}) custom-call(f32[768,128]{1,0:T(8,128)S(1)} %bitcast.13, f32[128,256]{1,0:T(8,128)S(1)} %get-tuple-element.17.value_ref, f32[128,256]{1,0:T(8,128)S(1)} %get-tuple-element.18.key_ref, f32[128,256]{1,0:T(8,128)S(1)} %get-tuple-element.19.cot_ref), custom_call_target="tpu_custom_call" | custom-call | tf_op jit(solution)/shard_map/pallas_call | solution.py:328
  (3 shorter events, 0.0 us)
Async XLA Ops:
  0.6 21.6 %copy-start.2 = (f32[17,2,8,128]{3,2,1,0:T(8,128)S(1)}, f32[17,2,8,128]{3,2,1,0:T(8,128)}, u32[]{:S(2)}) copy-start(f32[17,2,8,128]{3,2,1,0:T(8,128)} %constant.11.clone.rowfix_ref) | copy-start | bytes 417796
  0.6 21.6 %copy-start.3 = (f32[17,2,8,128]{3,2,1,0:T(8,128)S(1)}, f32[17,2,8,128]{3,2,1,0:T(8,128)}, u32[]{:S(2)}) copy-start(f32[17,2,8,128]{3,2,1,0:T(8,128)} %constant.10.clone.twiddle_ref) | copy-start | bytes 417796
  1.9 20.3 %copy-start = (bf16[512,256]{1,0:T(8,128)(2,1)S(1)}, bf16[512,256]{1,0:T(8,128)(2,1)}, u32[]{:S(2)}) copy-start(bf16[512,256]{1,0:T(8,128)(2,1)} %constant.9.clone.inverse_ref) | copy-start | bytes 786436
  1.9 20.3 %copy-start.1 = (bf16[512,256]{1,0:T(8,128)(2,1)S(1)}, bf16[512,256]{1,0:T(8,128)(2,1)}, u32[]{:S(2)}) copy-start(bf16[512,256]{1,0:T(8,128)(2,1)} %constant.8.clone.forward_ref) | copy-start | bytes 786436
  23.0 5.0 %collective-permute-start = (f32[64,128]{1,0:T(8,128)S(1)}, f32[64,128]{1,0:T(8,128)S(1)}, u32[]{:S(2)}, u32[]{:S(2)}) collective-permute-start(f32[64,128]{1,0:T(8,128)S(1)} %get-tuple-element.15), channel_id=1, source_target_pairs={{0,193},{1,64},{64,1},{65,128},{128,65},{129,192},{192,129},{193,0... | collective-permute-start | bytes 98312 | tf_op jit(solution)/shard_map/ppermute | solution.py:322
  28.0 6.5 %collective-permute-start.1 = (f32[64,128]{1,0:T(8,128)S(1)}, f32[64,128]{1,0:T(8,128)S(1)}, u32[]{:S(2)}, u32[]{:S(2)}) collective-permute-start(f32[64,128]{1,0:T(8,128)S(1)} %add.6), channel_id=1, source_target_pairs={{0,65},{1,192},{64,129},{65,0},{128,193},{129,64},{192,1},{193,128... | collective-permute-start | bytes 98312 | tf_op jit(solution)/shard_map/ppermute | solution.py:322

commit v9 on v7

--- a/solution.py
+++ b/solution.py
@@ -315,12 +315,12 @@
     spec, part = call(forward_kernel, [(544, 256), (64, 128)], 5, [(680, 256)])(
         signal, forward, inverse, twiddle, rowfix
     )
-    for pairs in STEPS:
-        part = part + lax.ppermute(part, ("zh", "core"), pairs)
+    part = part + lax.ppermute(part, ("zh", "core"), STEPS[0])
+    more = lax.ppermute(part, ("zh", "core"), STEPS[1])
     (message,) = call(inverse_kernel, [(768, 128)], 6, [(680, 256)] * 2 + [(128, 128)])(
         signal, spec, forward, inverse, twiddle, rowfix
     )
-    (message,) = call(filter_kernel, [(768, 128)], 2)(part, message)
+    (message,) = call(filter_kernel, [(768, 128)], 3)(part, more, message)
     signal = exchange(message.reshape(64, 1, 1536), FAR).reshape(768, 128)
     query_grad, key_grad, value_grad, filter_grad = call(unpack_kernel, [shape] * 4, 4)(signal, value, key, cot)
     return query_grad[None], key_grad[None], value_grad[None], filter_grad

time: 50.3 us -> 50.3 us (level)
  no operation moved by 1% of the time
where the time goes in v9:
time: 50.3 us; the launch traced here: 50.1 us
  blocking collectives  35 us (70%)
  starting transfers between devices  8.21 us (16%)
  Pallas kernels  3.7 us (7%)
  waiting for transfers between devices  2.43 us (5%)
  between operations  0.71 us (1%)
    all_to_all x2, blocking collectives, exchange(): return lax.all_to_all(array, axes, split_axis=0, concat_axis=0, tiled=True)  35 us
    ppermute x1, starting transfers between devices, on_device(): more = lax.ppermute(part, ('zh', 'core'), STEPS[1])  4.86 us
    ppermute x1, starting transfers between devices, on_device(): part = part + lax.ppermute(part, ('zh', 'core'), STEPS[0])  3.36 us
    ppermute x1, waiting for transfers between devices, on_device(): part = part + lax.ppermute(part, ('zh', 'core'), STEPS[0])  1.6 us
    pallas_call x1, Pallas kernels, on_device(): call(pack_kernel, [(576, 128)] + [shape] * 3, 5, [shape, (2, 32, 128)], c...  1.22 us
  transfers between devices with their start and end apart: 2, of which 2 were waited for; matrix products, arithmetic and copies ran while one was open for 0% of the time, Pallas kernels for 2%

profile of v9, /device:TPU:1, one launch (start us, length us, event | category | flops | bytes accessed | tf_op | source)
XLA Modules:
  0.0 50.1 jit_solution(3372610789830060846)
XLA Ops:
  0.6 0.0 copy-start.1
  0.6 0.0 copy-start.3
  0.7 1.2 %shard_map.120 = (f32[576,128]{1,0:T(8,128)S(1)}, f32[128,256]{1,0:T(8,128)S(1)}, f32[128,256]{1,0:T(8,128)S(1)}, f32[128,256]{1,0:T(8,128)S(1)}) custom-call(f32[128,256]{1,0:T(8,128)} %bitcast.16, f32[128,256]{1,0:T(8,128)} %bitcast.17, f32[128,256]{1,0:T(8,128)} %bitcast.18, f32[128,256]{1,0:T(8,128)} %bitcast.19, f32[128,256]{1,0:T(8,128)} %filter_hbm.1), custom_call_target="tpu_custom_call" | custom-call | tf_op jit(solution)/shard_map/pallas_call | solution.py:313
  1.9 0.0 copy-start
  1.9 0.0 copy-start.2
  1.9 20.3 %all_to_all.10 = f32[64,1,1152]{2,1,0:T(1,128)S(1)} all-to-all(f32[64,1,1152]{2,1,0:T(1,128)S(1)} %bitcast.15), channel_id=1, replica_groups=mesh['zh'=4,'y'=4,'x'=4,'zl'=2,'core'=2] {'zl','x','y','core'}, dimensions={0} | all-to-all | bytes 589824 | tf_op jit(solution)/shard_map/all_to_all | solution.py:305
  22.2 0.0 copy-done.1
  22.2 0.0 copy-done.3
  22.2 0.0 copy-done
  22.2 0.0 copy-done.2
  22.2 0.8 %shard_map.121 = (f32[544,256]{1,0:T(8,128)S(1)}, f32[64,128]{1,0:T(8,128)S(1)}) custom-call(f32[576,128]{1,0:T(8,128)S(1)} %bitcast.11, bf16[768,256]{1,0:T(8,128)(2,1)S(1)} %copy-done.1, bf16[768,256]{1,0:T(8,128)(2,1)S(1)} %copy-done, f32[17,2,8,128]{3,2,1,0:T(8,128)S(1)} %copy-done.3, f32[17,2,8,128]{3,2,1,0:T(8,128)S(1)} %copy-done.2), custom_call_target="tpu_custom_call" | custom-call | tf_op jit(solution)/shard_map/pallas_call | solution.py:315
  23.1 3.4 %collective-permute-start = (f32[64,128]{1,0:T(8,128)S(1)}, f32[64,128]{1,0:T(8,128)S(1)}, u32[]{:S(2)}, u32[]{:S(2)}) collective-permute-start(f32[64,128]{1,0:T(8,128)S(1)} %get-tuple-element.15), channel_id=1, source_target_pairs={{0,193},{1,64},{64,1},{65,128},{128,65},{129,192},{192,129},{193,0... | collective-permute-start | bytes 98312 | tf_op jit(solution)/shard_map/ppermute | solution.py:318
  26.4 1.6 %collective-permute-done = f32[64,128]{1,0:T(8,128)S(1)} collective-permute-done((f32[64,128]{1,0:T(8,128)S(1)}, f32[64,128]{1,0:T(8,128)S(1)}, u32[]{:S(2)}, u32[]{:S(2)}) %collective-permute-start) | collective-permute-done | bytes 32800 | tf_op jit(solution)/shard_map/ppermute | solution.py:318
  28.0 4.9 %collective-permute-start.1 = (f32[64,128]{1,0:T(8,128)S(1)}, f32[64,128]{1,0:T(8,128)S(1)}, u32[]{:S(2)}, u32[]{:S(2)}) collective-permute-start(f32[64,128]{1,0:T(8,128)S(1)} %add.3.part_ref), channel_id=1, source_target_pairs={{0,65},{1,192},{64,129},{65,0},{128,193},{129,64},{192,1},{193,128... | collective-permute-start | bytes 98312 | tf_op jit(solution)/shard_map/ppermute | solution.py:319
  32.9 0.8 %shard_map.122.refs_1_ = f32[768,128]{1,0:T(8,128)S(1)} custom-call(f32[576,128]{1,0:T(8,128)S(1)} %bitcast.12, f32[544,256]{1,0:T(8,128)S(1)} %get-tuple-element.16.spec_ref, bf16[768,256]{1,0:T(8,128)(2,1)S(1)} %copy-done.1, bf16[768,256]{1,0:T(8,128)(2,1)S(1)} %copy-done, f32[17,2,8,128]{3,2,1,0:T(8,128)S(1)} %copy-done.3, f32[17,2,8,128]{3,2,1,0:T(8,128)S(1)} %copy-done.2), custom_call_target="tpu_custom_call" | custom-call | tf_op jit(solution)/shard_map/pallas_call | solution.py:320
  33.6 0.8 %collective-permute-done.1.refs_0_ = f32[64,128]{1,0:T(8,128)S(1)} collective-permute-done((f32[64,128]{1,0:T(8,128)S(1)}, f32[64,128]{1,0:T(8,128)S(1)}, u32[]{:S(2)}, u32[]{:S(2)}) %collective-permute-start.1) | collective-permute-done | bytes 32800 | tf_op jit(solution)/shard_map/ppermute | solution.py:319
  34.5 14.7 %all_to_all.11 = f32[64,1,1536]{2,1,0:T(1,128)S(1)} all-to-all(f32[64,1,1536]{2,1,0:T(1,128)S(1)} %bitcast.14), channel_id=1, replica_groups=mesh['zh'=4,'y'=4,'x'=4,'zl'=2,'core'=2] {'zl','x','y','core'}, dimensions={0} | all-to-all | bytes 786432 | tf_op jit(solution)/shard_map/all_to_all | solution.py:305
  49.2 0.9 %shard_map.124 = (f32[128,256]{1,0:T(8,128)}, f32[128,256]{1,0:T(8,128)}, f32[128,256]{1,0:T(8,128)}, f32[128,256]{1,0:T(8,128)}) custom-call(f32[768,128]{1,0:T(8,128)S(1)} %bitcast.13, f32[128,256]{1,0:T(8,128)S(1)} %get-tuple-element.17.value_ref, f32[128,256]{1,0:T(8,128)S(1)} %get-tuple-element.18.key_ref, f32[128,256]{1,0:T(8,128)S(1)} %get-tuple-element.19.cot_ref), custom_call_target="tpu_custom_call" | custom-call | tf_op jit(solution)/shard_map/pallas_call | solution.py:325
  (2 shorter events, 0.0 us)
Async XLA Ops:
  0.6 21.6 %copy-start.1 = (bf16[768,256]{1,0:T(8,128)(2,1)S(1)}, bf16[768,256]{1,0:T(8,128)(2,1)}, u32[]{:S(2)}) copy-start(bf16[768,256]{1,0:T(8,128)(2,1)} %constant.8.clone.forward_ref) | copy-start | bytes 1179652
  0.6 21.6 %copy-start.3 = (f32[17,2,8,128]{3,2,1,0:T(8,128)S(1)}, f32[17,2,8,128]{3,2,1,0:T(8,128)}, u32[]{:S(2)}) copy-start(f32[17,2,8,128]{3,2,1,0:T(8,128)} %constant.10.clone.twiddle_ref) | copy-start | bytes 417796
  1.9 20.3 %copy-start = (bf16[768,256]{1,0:T(8,128)(2,1)S(1)}, bf16[768,256]{1,0:T(8,128)(2,1)}, u32[]{:S(2)}) copy-start(bf16[768,256]{1,0:T(8,128)(2,1)} %constant.9.clone.inverse_ref) | copy-start | bytes 1179652
  1.9 20.3 %copy-start.2 = (f32[17,2,8,128]{3,2,1,0:T(8,128)S(1)}, f32[17,2,8,128]{3,2,1,0:T(8,128)}, u32[]{:S(2)}) copy-start(f32[17,2,8,128]{3,2,1,0:T(8,128)} %constant.11.clone.rowfix_ref) | copy-start | bytes 417796
  23.1 5.0 %collective-permute-start = (f32[64,128]{1,0:T(8,128)S(1)}, f32[64,128]{1,0:T(8,128)S(1)}, u32[]{:S(2)}, u32[]{:S(2)}) collective-permute-start(f32[64,128]{1,0:T(8,128)S(1)} %get-tuple-element.15), channel_id=1, source_target_pairs={{0,193},{1,64},{64,1},{65,128},{128,65},{129,192},{192,129},{193,0... | collective-permute-start | bytes 98312 | tf_op jit(solution)/shard_map/ppermute | solution.py:318
  28.0 6.5 %collective-permute-start.1 = (f32[64,128]{1,0:T(8,128)S(1)}, f32[64,128]{1,0:T(8,128)S(1)}, u32[]{:S(2)}, u32[]{:S(2)}) collective-permute-start(f32[64,128]{1,0:T(8,128)S(1)} %add.3.part_ref), channel_id=1, source_target_pairs={{0,65},{1,192},{64,129},{65,0},{128,193},{129,64},{192,1},{193,128... | collective-permute-start | bytes 98312 | tf_op jit(solution)/shard_map/ppermute | solution.py:319
